TPU v7x, 128 devices: a whole 4x4x4 slice. The times are simulated.
128 devices in a mesh: slab: 32 (over z, x, core), sub: 4 (over y).
Axes of the slice: x: 4, y: 4, z: 4, core: 2. Of those that a mesh axis runs over, the one named last changes fastest.
Arguments:
- leaves: bfloat16 [65536, 152], P(('slab', 'sub')), may hold values from -6 to 6
- coarse_local: bfloat16 [8192, 152], P(('slab', 'sub')), may hold values from -6 to 6
- m2m: bfloat16 [8, 152, 152], replicated, may hold values from -0.15625 to 0.15625
- m2l: bfloat16 [316, 152, 152], replicated, may hold values from -0.5 to 0.5
- c2e: float32 [152, 152], replicated, may hold values from -0.0625 to 0.0625
- l2l: bfloat16 [8, 152, 152], replicated, may hold values from -0.5 to 0.5
- send_box: int32 [128, 2560], P(('slab', 'sub')), may hold values from -1 to 63, as said below
- pair_box: int32 [525824], P(('slab', 'sub')), may hold values from 0 to 63, as said below
- pair_partner: int32 [525824], P(('slab', 'sub')), may hold values from -1 to 2623, as said below
- pair_op: int32 [525824], P(('slab', 'sub')), may hold values from 0 to 315, as said below
Outputs:
- parent_local: bfloat16 [8192, 152], P(('slab', 'sub'))
- leaf_local: float32 [65536, 152], P(('slab', 'sub'))
Inputs may be any that keep to these rules, and one draw needn't show every extreme that they name: `send_box`: row q, column r * 20 + k: the index among device q's own 64 level-6 boxes of the k-th box whose density device r needs, or -1. In each (q, r) the entries other than -1 come first; q = r is all -1. In every draw one device sends 20 boxes to every other device and receives 20 from every other device. `pair_box`: entry r * 4108 + i: the own box, among device r's 64, of slot i of device r's list. `pair_partner`: entry r * 4108 + i: -1 for a padded slot (padded slots may stand anywhere); below 64: another own box of device r; else 64 + q * 20 + k, the slot k that device q fills for device r, which is not -1 in send_box. In every draw one device has no padded slot and another has 2054 of them, and some live slot names the last row of its table. `pair_op`: A device's 4108 entries form 316 aligned runs of 13 equal ids, and every id fills exactly one run of each device. Id 316 - 1 - k is the opposite vector of id k.
All inputs are finite; a program needn't handle non-finite values.
Results may differ from a plain program's by a relative error of at most 0.0075.
Values may be sent and summed in bfloat16 or wider, within the bound.
No kernel may reach another device: no remote copies, remote signals or barrier semaphores. Data moves between devices by JAX's collectives and lax.ppermute only.
A program may use at most 128 MiB of HBM per device.

v0:
```python
import jax
import jax.numpy as jnp
from jax import lax
from jax.sharding import PartitionSpec as P

NOPS = 316
CAP = 20
LEAD = 300
OPCAP = 13


def shifted(x, axis, by):
    count = lax.axis_size(axis)
    return lax.ppermute(x, axis, [(i, (i + by) % count) for i in range(count)])


def contract_rows(picker, values, precision):
    return lax.dot_general(
        picker,
        values,
        (((0,), (0,)), ((), ())),
        precision=precision,
        preferred_element_type=jnp.float32,
    )


def shards(leaves, coarse_local, m2m, m2l, c2e, l2l, send_box, pair_box, pair_partner, pair_op):
    n_slab = lax.axis_size("slab")
    n_sub = lax.axis_size("sub")
    devices = n_slab * n_sub
    width_dens = leaves.shape[1]
    box_count = leaves.shape[0] // 8
    edge_boxes = (LEAD + 7) // 8
    front = jnp.concatenate(
        [jnp.zeros((8 * edge_boxes - LEAD, width_dens), leaves.dtype), leaves[:LEAD]]
    )
    front_sum = jnp.einsum(
        "poj,oji->pi",
        front.reshape(edge_boxes, 8, width_dens),
        m2m,
        preferred_element_type=jnp.float32,
    )
    arrived = shifted(front_sum, ("slab", "sub"), -1)
    own_rows = jnp.concatenate([leaves[LEAD:], jnp.zeros((LEAD, width_dens), leaves.dtype)])
    up_sum = jnp.einsum(
        "poj,oji->pi",
        own_rows.reshape(box_count, 8, width_dens),
        m2m,
        preferred_element_type=jnp.float32,
    )
    up_sum = up_sum.at[box_count - edge_boxes :].add(arrived)
    upward = up_sum.astype(jnp.bfloat16)
    send_slots = send_box.reshape(devices, CAP)
    slot_live = send_slots >= 0
    outgoing = jnp.where(
        slot_live[:, :, None], upward[jnp.maximum(send_slots, 0)], jnp.zeros((), jnp.bfloat16)
    )
    incoming = lax.all_to_all(outgoing, ("slab", "sub"), split_axis=0, concat_axis=0, tiled=True)
    table_rows = jnp.concatenate([upward, incoming.reshape(devices * CAP, width_dens)])
    table_count = table_rows.shape[0]
    per_block = NOPS // 4
    block_rows = per_block * OPCAP
    run_ids = pair_op.reshape(NOPS, OPCAP)[:, 0]
    in_use = pair_partner >= 0
    source_rows = jnp.where(in_use, pair_partner, -1)
    owner_slots = jnp.where(in_use, pair_box, -1)
    table_iota = jnp.arange(table_count, dtype=jnp.int32)
    box_iota = jnp.arange(box_count, dtype=jnp.int32)

    def block_step(index, carry):
        own_total, table_total = carry
        first = index * block_rows
        sources = lax.dynamic_slice_in_dim(source_rows, first, block_rows)
        owners = lax.dynamic_slice_in_dim(owner_slots, first, block_rows)
        ids = lax.dynamic_slice_in_dim(run_ids, index * per_block, per_block)
        pick_table = (sources[:, None] == table_iota[None, :]).astype(jnp.bfloat16)
        pick_owner = (owners[:, None] == box_iota[None, :]).astype(jnp.bfloat16)
        partner_dens = jnp.dot(pick_table, table_rows, preferred_element_type=jnp.float32).astype(
            jnp.bfloat16
        )
        owner_dens = jnp.dot(pick_owner, upward, preferred_element_type=jnp.float32).astype(
            jnp.bfloat16
        )
        toward_owner = jnp.einsum(
            "kcj,kji->kci",
            partner_dens.reshape(per_block, OPCAP, width_dens),
            m2l[ids],
            preferred_element_type=jnp.float32,
        ).reshape(block_rows, width_dens)
        toward_partner = jnp.einsum(
            "kcj,kji->kci",
            owner_dens.reshape(per_block, OPCAP, width_dens),
            m2l[NOPS - 1 - ids],
            preferred_element_type=jnp.float32,
        ).reshape(block_rows, width_dens)
        own_total = own_total + contract_rows(
            pick_owner.astype(jnp.float32), toward_owner, lax.Precision.HIGHEST
        )
        high_part = toward_partner.astype(jnp.bfloat16)
        low_part = (toward_partner - high_part.astype(jnp.float32)).astype(jnp.bfloat16)
        table_total = (
            table_total
            + contract_rows(pick_table, high_part, None)
            + contract_rows(pick_table, low_part, None)
        )
        return (own_total, table_total)

    start_carry = (
        jnp.zeros((box_count, width_dens), jnp.float32),
        jnp.zeros((table_count, width_dens), jnp.float32),
    )
    own_total, table_total = lax.fori_loop(0, 4, block_step, start_carry)
    to_owners = table_total[box_count:]
    came_back = lax.all_to_all(
        to_owners.reshape(devices, CAP, width_dens).astype(jnp.bfloat16),
        ("slab", "sub"),
        split_axis=0,
        concat_axis=0,
        tiled=True,
    ).astype(jnp.float32)
    owner_rows = jnp.where(slot_live, send_slots, box_count).reshape(-1)
    returned = jax.ops.segment_sum(
        came_back.reshape(devices * CAP, width_dens), owner_rows, num_segments=box_count + 1
    )
    check = own_total + table_total[:box_count] + returned[:box_count]
    parent_local = (
        jnp.dot(check, c2e, precision=lax.Precision.HIGHEST, preferred_element_type=jnp.float32)
        + coarse_local.astype(jnp.float32)
    ).astype(jnp.bfloat16)
    earlier = shifted(parent_local[box_count - edge_boxes :], ("slab", "sub"), 1)
    head = jnp.einsum("pj,oji->poi", earlier, l2l, preferred_element_type=jnp.float32).reshape(
        8 * edge_boxes, width_dens
    )
    own_part = jnp.einsum(
        "pj,oji->poi", parent_local, l2l, preferred_element_type=jnp.float32
    ).reshape(8 * box_count, width_dens)
    leaf_local = jnp.concatenate([head[8 * edge_boxes - LEAD :], own_part[: 8 * box_count - LEAD]])
    return (parent_local, leaf_local)


def solution(mesh):
    placed = (
        P(("slab", "sub"), None),
        P(("slab", "sub"), None),
        P(),
        P(),
        P(),
        P(),
        P(("slab", "sub"), None),
        P(("slab", "sub")),
        P(("slab", "sub")),
        P(("slab", "sub")),
    )
    return jax.shard_map(
        shards,
        mesh=mesh,
        in_specs=placed,
        out_specs=(P(("slab", "sub"), None), P(("slab", "sub"), None)),
        check_vma=False,
    )
```

profile of v0, /device:TPU:0, one launch (start us, length us, event | category | flops | bytes accessed | tf_op | source)
XLA Modules:
  0.0 358.3 jit_solution(7755707683609685299)
XLA Ops:
  1.9 1.3 convolution_bitcast_fusion.1
  3.2 8.3 %collective-permute-start = (f32[38,152]{1,0:T(8,128)S(1)}, f32[38,152]{1,0:T(8,128)S(1)}, u32[]{:S(2)}, u32[]{:S(2)}) collective-permute-start(f32[38,152]{1,0:T(8,128)S(1)} %convolution_bitcast_fusion.1), channel_id=1, source_target_pairs={{0,127},{1,0},{2,1},{3,2},{4,3},{5,4},{6,5},{7,6},{8,7},{9,8},{10,... | collective-permute-start | bytes 69320 | tf_op jit(solution)/shard_map/ppermute | solution.py:14
  13.5 7.6 %gather_fusion.2 = bf16[2560,152]{1,0:T(8,128)(2,1)S(1)} fusion(bf16[64,152]{1,0:T(8,128)(2,1)S(1)} %convert_element_type.73, s32[3072]{0:T(1024)S(1)} %pad_clamp_fusion.2), kind=kCustom, calls=%fused_computation.2 | custom fusion | bytes 1566720 | tf_op jit(solution)/shard_map/gather | solution.py:56
  21.1 1.4 reshape.169
  22.4 1.7 broadcast_select_fusion
  24.1 2.8 reshape.206
  26.9 9.1 %all-to-all-start = ((bf16[128,2,1520]{2,1,0:T(2,128)(2,1)}), bf16[128,2,1520]{2,1,0:T(2,128)(2,1)S(1)}, u32[]{:S(2)}, u32[]{:S(2)}) async-start(bf16[128,2,1520]{2,1,0:T(2,128)(2,1)} %reshape.206), calls=%async_computation | async-start | bytes 1572864 | tf_op jit(solution)/shard_map/all_to_all | solution.py:58
  36.1 37.1 %copy.23 = bf16[316,152,152]{2,1,0:T(8,128)(2,1)} copy(bf16[316,152,152]{0,2,1:T(8,128)(2,1)} %param.17) | data formatting | bytes 29203456
  74.2 2.2 reshape.207
  77.0 1.3 pad_maximum_fusion
  78.3 218.4 %while.19 = (s32[]{:T(128)}, f32[64,152]{1,0:T(8,128)}, f32[2624,152]{0,1:T(8,128)}, s32[4108]{0:T(1024)}, s32[4108]{0:T(1024)}, /*index=5*/bf16[2624,152]{1,0:T...) while((s32[]{:T(128)}, f32[64,152]{1,0:T(8,128)}, ...), condition=%wide.region_1.2_spmd.clone, body=%wide.region_0.0_spmd.clone.sunk | while | flops 2703009280 | bytes 51667552 | solution.py:112
  78.4 14.3 %gather_fusion.1 = bf16[79,152,152]{2,1,0:T(8,128)(2,1)} fusion(bf16[316,152,152]{2,1,0:T(8,128)(2,1)} %get-tuple-element.450, s32[1024]{0:T(1024)S(1)} %get-tuple-element.412), kind=kCustom, calls=%fused_computation.1.clone.clone.1 | custom fusion | bytes 7301180 | tf_op jit(solution)/shard_map/while/body/eval_jaxpr/gather | solution.py:93
  94.4 3.8 %fusion.64 = f32[79,13,152]{2,1,0:T(8,128)S(1)} fusion(bf16[79,13,152]{2,1,0:T(8,128)(2,1)S(1)} %reshape.224, bf16[79,152,152]{2,1,0:T(8,128)(2,1)} %gather_fusion.1), kind=kOutput, calls=%fused_computation.60.clone.1 | convolution fusion | flops 47455616 | bytes 4587056 | tf_op jit(solution)/shard_map/while/body/eval_jaxpr/kcj,kji->kci/dot_general | solution.py:90
  99.1 3.9 %fusion.65 = f32[2624,152]{0,1:T(8,128)} fusion(s32[1027]{0:T(1024)S(1)} %dynamic_slice.39, f32[1027,152]{1,0:T(8,128)S(1)} %reshape.225), kind=kOutput, calls=%fused_computation.7.clone.1 | convolution fusion | flops 822553088 | bytes 2223916 | tf_op jit(solution)/shard_map/while/body/eval_jaxpr/dot_general | solution.py:18
  103.1 4.5 %fusion.66 = f32[2624,152]{0,1:T(8,128)S(1)} fusion(f32[2624,152]{0,1:T(8,128)} %fusion.65, s32[1027]{0:T(1024)S(1)} %dynamic_slice.39, f32[2624,152]{0,1:T(8,128)S(1)} %copy-done.1, pred[]{:T(512)S(6)} %compare.10, f32[1027,152]{1,0:T(8,128)S(1)} %reshape.225), kind=kOutput, calls=%fused_computation.14.clone.1 | convolution fusion | flops 823281280 | bytes 5414701 | tf_op jit(solution)/shard_map/while/body/eval_jaxpr/dot_general | solution.py:18
  107.6 14.9 %gather_fusion = bf16[79,152,152]{2,1,0:T(8,128)(2,1)} fusion(bf16[316,152,152]{2,1,0:T(8,128)(2,1)} %get-tuple-element.450, s32[1024]{0:T(1024)S(1)} %get-tuple-element.411), kind=kCustom, calls=%fused_computation.clone.clone.1 | custom fusion | bytes 7301180 | tf_op jit(solution)/shard_map/while/body/eval_jaxpr/gather | solution.py:87
  122.5 3.9 %fusion.62 = bf16[1027,152]{0,1:T(8,128)(2,1)S(1)} fusion(bf16[2624,152]{1,0:T(8,128)(2,1)} %get-tuple-element.448, s32[1027]{0:T(1024)S(1)} %dynamic_slice.39), kind=kOutput, calls=%fused_computation.15.clone.1 | convolution fusion | flops 822084736 | bytes 1114012 | tf_op jit(solution)/shard_map/while/body/eval_jaxpr/dot_general | solution.py:78
  126.8 3.8 %fusion.63 = f32[79,13,152]{2,1,0:T(8,128)S(1)} fusion(bf16[79,13,152]{2,1,0:T(8,128)(2,1)S(1)} %reshape.222, bf16[79,152,152]{2,1,0:T(8,128)(2,1)} %gather_fusion), kind=kOutput, calls=%fused_computation.59.clone.1 | convolution fusion | flops 47455616 | bytes 4587056 | tf_op jit(solution)/shard_map/while/body/eval_jaxpr/kcj,kji->kci/dot_general | solution.py:84
  133.0 14.3 %gather_fusion.1 = bf16[79,152,152]{2,1,0:T(8,128)(2,1)} fusion(bf16[316,152,152]{2,1,0:T(8,128)(2,1)} %get-tuple-element.450, s32[1024]{0:T(1024)S(1)} %get-tuple-element.412), kind=kCustom, calls=%fused_computation.1.clone.clone.1 | custom fusion | bytes 7301180 | tf_op jit(solution)/shard_map/while/body/eval_jaxpr/gather | solution.py:93
  149.0 3.8 %fusion.64 = f32[79,13,152]{2,1,0:T(8,128)S(1)} fusion(bf16[79,13,152]{2,1,0:T(8,128)(2,1)S(1)} %reshape.224, bf16[79,152,152]{2,1,0:T(8,128)(2,1)} %gather_fusion.1), kind=kOutput, calls=%fused_computation.60.clone.1 | convolution fusion | flops 47455616 | bytes 4587056 | tf_op jit(solution)/shard_map/while/body/eval_jaxpr/kcj,kji->kci/dot_general | solution.py:90
  153.7 4.0 %fusion.65 = f32[2624,152]{0,1:T(8,128)} fusion(s32[1027]{0:T(1024)S(1)} %dynamic_slice.39, f32[1027,152]{1,0:T(8,128)S(1)} %reshape.225), kind=kOutput, calls=%fused_computation.7.clone.1 | convolution fusion | flops 822553088 | bytes 2223916 | tf_op jit(solution)/shard_map/while/body/eval_jaxpr/dot_general | solution.py:18
  157.7 4.5 %fusion.66 = f32[2624,152]{0,1:T(8,128)S(1)} fusion(f32[2624,152]{0,1:T(8,128)} %fusion.65, s32[1027]{0:T(1024)S(1)} %dynamic_slice.39, f32[2624,152]{0,1:T(8,128)S(1)} %copy-done.1, pred[]{:T(512)S(6)} %compare.10, f32[1027,152]{1,0:T(8,128)S(1)} %reshape.225), kind=kOutput, calls=%fused_computation.14.clone.1 | convolution fusion | flops 823281280 | bytes 5414701 | tf_op jit(solution)/shard_map/while/body/eval_jaxpr/dot_general | solution.py:18
  162.2 14.9 %gather_fusion = bf16[79,152,152]{2,1,0:T(8,128)(2,1)} fusion(bf16[316,152,152]{2,1,0:T(8,128)(2,1)} %get-tuple-element.450, s32[1024]{0:T(1024)S(1)} %get-tuple-element.411), kind=kCustom, calls=%fused_computation.clone.clone.1 | custom fusion | bytes 7301180 | tf_op jit(solution)/shard_map/while/body/eval_jaxpr/gather | solution.py:87
  177.1 3.9 %fusion.62 = bf16[1027,152]{0,1:T(8,128)(2,1)S(1)} fusion(bf16[2624,152]{1,0:T(8,128)(2,1)} %get-tuple-element.448, s32[1027]{0:T(1024)S(1)} %dynamic_slice.39), kind=kOutput, calls=%fused_computation.15.clone.1 | convolution fusion | flops 822084736 | bytes 1114012 | tf_op jit(solution)/shard_map/while/body/eval_jaxpr/dot_general | solution.py:78
  181.4 3.8 %fusion.63 = f32[79,13,152]{2,1,0:T(8,128)S(1)} fusion(bf16[79,13,152]{2,1,0:T(8,128)(2,1)S(1)} %reshape.222, bf16[79,152,152]{2,1,0:T(8,128)(2,1)} %gather_fusion), kind=kOutput, calls=%fused_computation.59.clone.1 | convolution fusion | flops 47455616 | bytes 4587056 | tf_op jit(solution)/shard_map/while/body/eval_jaxpr/kcj,kji->kci/dot_general | solution.py:84
  187.6 14.3 %gather_fusion.1 = bf16[79,152,152]{2,1,0:T(8,128)(2,1)} fusion(bf16[316,152,152]{2,1,0:T(8,128)(2,1)} %get-tuple-element.450, s32[1024]{0:T(1024)S(1)} %get-tuple-element.412), kind=kCustom, calls=%fused_computation.1.clone.clone.1 | custom fusion | bytes 7301180 | tf_op jit(solution)/shard_map/while/body/eval_jaxpr/gather | solution.py:93
  203.6 3.8 %fusion.64 = f32[79,13,152]{2,1,0:T(8,128)S(1)} fusion(bf16[79,13,152]{2,1,0:T(8,128)(2,1)S(1)} %reshape.224, bf16[79,152,152]{2,1,0:T(8,128)(2,1)} %gather_fusion.1), kind=kOutput, calls=%fused_computation.60.clone.1 | convolution fusion | flops 47455616 | bytes 4587056 | tf_op jit(solution)/shard_map/while/body/eval_jaxpr/kcj,kji->kci/dot_general | solution.py:90
  208.3 4.0 %fusion.65 = f32[2624,152]{0,1:T(8,128)} fusion(s32[1027]{0:T(1024)S(1)} %dynamic_slice.39, f32[1027,152]{1,0:T(8,128)S(1)} %reshape.225), kind=kOutput, calls=%fused_computation.7.clone.1 | convolution fusion | flops 822553088 | bytes 2223916 | tf_op jit(solution)/shard_map/while/body/eval_jaxpr/dot_general | solution.py:18
  212.3 4.5 %fusion.66 = f32[2624,152]{0,1:T(8,128)S(1)} fusion(f32[2624,152]{0,1:T(8,128)} %fusion.65, s32[1027]{0:T(1024)S(1)} %dynamic_slice.39, f32[2624,152]{0,1:T(8,128)S(1)} %copy-done.1, pred[]{:T(512)S(6)} %compare.10, f32[1027,152]{1,0:T(8,128)S(1)} %reshape.225), kind=kOutput, calls=%fused_computation.14.clone.1 | convolution fusion | flops 823281280 | bytes 5414701 | tf_op jit(solution)/shard_map/while/body/eval_jaxpr/dot_general | solution.py:18
  216.8 14.9 %gather_fusion = bf16[79,152,152]{2,1,0:T(8,128)(2,1)} fusion(bf16[316,152,152]{2,1,0:T(8,128)(2,1)} %get-tuple-element.450, s32[1024]{0:T(1024)S(1)} %get-tuple-element.411), kind=kCustom, calls=%fused_computation.clone.clone.1 | custom fusion | bytes 7301180 | tf_op jit(solution)/shard_map/while/body/eval_jaxpr/gather | solution.py:87
  231.7 3.9 %fusion.62 = bf16[1027,152]{0,1:T(8,128)(2,1)S(1)} fusion(bf16[2624,152]{1,0:T(8,128)(2,1)} %get-tuple-element.448, s32[1027]{0:T(1024)S(1)} %dynamic_slice.39), kind=kOutput, calls=%fused_computation.15.clone.1 | convolution fusion | flops 822084736 | bytes 1114012 | tf_op jit(solution)/shard_map/while/body/eval_jaxpr/dot_general | solution.py:78
  236.1 3.8 %fusion.63 = f32[79,13,152]{2,1,0:T(8,128)S(1)} fusion(bf16[79,13,152]{2,1,0:T(8,128)(2,1)S(1)} %reshape.222, bf16[79,152,152]{2,1,0:T(8,128)(2,1)} %gather_fusion), kind=kOutput, calls=%fused_computation.59.clone.1 | convolution fusion | flops 47455616 | bytes 4587056 | tf_op jit(solution)/shard_map/while/body/eval_jaxpr/kcj,kji->kci/dot_general | solution.py:84
  242.2 14.3 %gather_fusion.1 = bf16[79,152,152]{2,1,0:T(8,128)(2,1)} fusion(bf16[316,152,152]{2,1,0:T(8,128)(2,1)} %get-tuple-element.450, s32[1024]{0:T(1024)S(1)} %get-tuple-element.412), kind=kCustom, calls=%fused_computation.1.clone.clone.1 | custom fusion | bytes 7301180 | tf_op jit(solution)/shard_map/while/body/eval_jaxpr/gather | solution.py:93
  258.2 3.8 %fusion.64 = f32[79,13,152]{2,1,0:T(8,128)S(1)} fusion(bf16[79,13,152]{2,1,0:T(8,128)(2,1)S(1)} %reshape.224, bf16[79,152,152]{2,1,0:T(8,128)(2,1)} %gather_fusion.1), kind=kOutput, calls=%fused_computation.60.clone.1 | convolution fusion | flops 47455616 | bytes 4587056 | tf_op jit(solution)/shard_map/while/body/eval_jaxpr/kcj,kji->kci/dot_general | solution.py:90
  262.9 4.0 %fusion.65 = f32[2624,152]{0,1:T(8,128)} fusion(s32[1027]{0:T(1024)S(1)} %dynamic_slice.39, f32[1027,152]{1,0:T(8,128)S(1)} %reshape.225), kind=kOutput, calls=%fused_computation.7.clone.1 | convolution fusion | flops 822553088 | bytes 2223916 | tf_op jit(solution)/shard_map/while/body/eval_jaxpr/dot_general | solution.py:18
  266.9 4.5 %fusion.66 = f32[2624,152]{0,1:T(8,128)S(1)} fusion(f32[2624,152]{0,1:T(8,128)} %fusion.65, s32[1027]{0:T(1024)S(1)} %dynamic_slice.39, f32[2624,152]{0,1:T(8,128)S(1)} %copy-done.1, pred[]{:T(512)S(6)} %compare.10, f32[1027,152]{1,0:T(8,128)S(1)} %reshape.225), kind=kOutput, calls=%fused_computation.14.clone.1 | convolution fusion | flops 823281280 | bytes 5414701 | tf_op jit(solution)/shard_map/while/body/eval_jaxpr/dot_general | solution.py:18
  271.4 14.9 %gather_fusion = bf16[79,152,152]{2,1,0:T(8,128)(2,1)} fusion(bf16[316,152,152]{2,1,0:T(8,128)(2,1)} %get-tuple-element.450, s32[1024]{0:T(1024)S(1)} %get-tuple-element.411), kind=kCustom, calls=%fused_computation.clone.clone.1 | custom fusion | bytes 7301180 | tf_op jit(solution)/shard_map/while/body/eval_jaxpr/gather | solution.py:87
  286.3 3.9 %fusion.62 = bf16[1027,152]{0,1:T(8,128)(2,1)S(1)} fusion(bf16[2624,152]{1,0:T(8,128)(2,1)} %get-tuple-element.448, s32[1027]{0:T(1024)S(1)} %dynamic_slice.39), kind=kOutput, calls=%fused_computation.15.clone.1 | convolution fusion | flops 822084736 | bytes 1114012 | tf_op jit(solution)/shard_map/while/body/eval_jaxpr/dot_general | solution.py:78
  290.7 3.8 %fusion.63 = f32[79,13,152]{2,1,0:T(8,128)S(1)} fusion(bf16[79,13,152]{2,1,0:T(8,128)(2,1)S(1)} %reshape.222, bf16[79,152,152]{2,1,0:T(8,128)(2,1)} %gather_fusion), kind=kOutput, calls=%fused_computation.59.clone.1 | convolution fusion | flops 47455616 | bytes 4587056 | tf_op jit(solution)/shard_map/while/body/eval_jaxpr/kcj,kji->kci/dot_general | solution.py:84
  296.7 1.7 slice.80
  299.4 2.7 reshape.208
  302.1 9.8 %all-to-all-start.1 = ((bf16[128,2,1520]{2,1,0:T(2,128)(2,1)}), bf16[128,2,1520]{2,1,0:T(2,128)(2,1)S(1)}, u32[]{:S(2)}, u32[]{:S(2)}) async-start(bf16[128,2,1520]{2,1,0:T(2,128)(2,1)} %reshape.208), calls=%async_computation.1 | async-start | bytes 1572864 | tf_op jit(solution)/shard_map/all_to_all | solution.py:114
  311.9 3.1 copy.24
  315.1 12.8 %all-to-all-done.1 = bf16[128,2,1520]{2,1,0:T(2,128)(2,1)S(1)} async-done(((bf16[128,2,1520]{2,1,0:T(2,128)(2,1)}), bf16[128,2,1520]{2,1,0:T(2,128)(2,1)S(1)}, u32[]{:S(2)}, u32[]{:S(2)}) %all-to-all-start.1) | async-done | bytes 778272 | tf_op jit(solution)/shard_map/all_to_all | solution.py:114
  327.9 2.2 reshape.209
  330.1 1.8 reshape.180
  331.9 15.3 %scatter_custom_fusion = f32[65,152]{1,0:T(8,128)S(1)} fusion(s32[2560]{0:T(1024)S(1)} %fusion.26, f32[2560,152]{1,0:T(8,128)} %reshape.180, f32[]{:T(128)} %constant.115.clone.1), kind=kCustom, calls=%fused_computation.48 | custom fusion | flops 389120 | bytes 40032 | tf_op jit(solution)/shard_map/scatter-add | solution.py:122
  349.6 7.4 %collective-permute-done.1 = bf16[38,152]{1,0:T(8,128)(2,1)S(1)} collective-permute-done((bf16[38,152]{1,0:T(8,128)(2,1)S(1)}, bf16[38,152]{1,0:T(8,128)(2,1)S(1)}, u32[]{:S(2)}, u32[]{:S(2)}) %collective-permute-start.1) | collective-permute-done | bytes 11584 | tf_op jit(solution)/shard_map/ppermute | solution.py:14
  (138 shorter events, 31.1 us)
Async XLA Ops:
  0.6 348.4 %copy-start = (bf16[8,152,152]{2,1,0:T(8,128)(2,1)S(1)}, bf16[8,152,152]{2,1,0:T(8,128)(2,1)}, u32[]{:S(2)}) copy-start(bf16[8,152,152]{2,1,0:T(8,128)(2,1)} %param.19) | copy-start | bytes 1108996
  0.6 10.9 %copy-start.7 = (bf16[512,152]{0,1:T(8,128)(2,1)S(1)}, bf16[512,152]{0,1:T(8,128)(2,1)}, u32[]{:S(2)}) copy-start(bf16[512,152]{0,1:T(8,128)(2,1)} %param.14) | copy-start | bytes 466948
  0.7 11.2 %copy-start.3 = (bf16[8,152,152]{2,1,0:T(8,128)(2,1)S(1)}, bf16[8,152,152]{2,1,0:T(8,128)(2,1)}, u32[]{:S(2)}) copy-start(bf16[8,152,152]{2,1,0:T(8,128)(2,1)} %param.16) | copy-start | bytes 1108996
  0.7 10.9 %copy-start.10 = (s32[1,2560]{1,0:T(1,128)S(1)}, s32[1,2560]{1,0:T(1,128)}, u32[]{:S(2)}) copy-start(s32[1,2560]{1,0:T(1,128)} %param.20) | copy-start | bytes 30724
  3.2 10.0 %collective-permute-start = (f32[38,152]{1,0:T(8,128)S(1)}, f32[38,152]{1,0:T(8,128)S(1)}, u32[]{:S(2)}, u32[]{:S(2)}) collective-permute-start(f32[38,152]{1,0:T(8,128)S(1)} %convolution_bitcast_fusion.1), channel_id=1, source_target_pairs={{0,127},{1,0},{2,1},{3,2},{4,3},{5,4},{6,5},{7,6},{8,7},{9,8},{10,... | collective-permute-start | bytes 69320 | tf_op jit(solution)/shard_map/ppermute | solution.py:14
  26.9 47.3 %all-to-all-start = ((bf16[128,2,1520]{2,1,0:T(2,128)(2,1)}), bf16[128,2,1520]{2,1,0:T(2,128)(2,1)S(1)}, u32[]{:S(2)}, u32[]{:S(2)}) async-start(bf16[128,2,1520]{2,1,0:T(2,128)(2,1)} %reshape.206), calls=%async_computation | async-start | bytes 1572864 | tf_op jit(solution)/shard_map/all_to_all | solution.py:58
  36.1 37.1 %copy-start.14 = (s32[4108]{0:T(1024)S(1)}, s32[4108]{0:T(1024)}, u32[]{:S(2)}) copy-start(s32[4108]{0:T(1024)} %param.23) | copy-start | bytes 49300
  36.1 37.5 %copy-start.12 = (s32[4108]{0:T(1024)S(1)}, s32[4108]{0:T(1024)}, u32[]{:S(2)}) copy-start(s32[4108]{0:T(1024)} %param.22) | copy-start | bytes 49300
  36.1 37.5 %copy-start.13 = (s32[4108]{0:T(1024)S(1)}, s32[4108]{0:T(1024)}, u32[]{:S(2)}) copy-start(s32[4108]{0:T(1024)} %param.21) | copy-start | bytes 49300
  99.1 4.0 %copy-start.1 = (f32[2624,152]{0,1:T(8,128)S(1)}, f32[2624,152]{0,1:T(8,128)}, u32[]{:S(2)}) copy-start(f32[2624,152]{0,1:T(8,128)} %get-tuple-element.430) | copy-start | bytes 4786180 | tf_op jit(solution)/shard_map/while
  107.5 14.9 %copy-start.2 = (f32[2624,152]{0,1:T(8,128)}, f32[2624,152]{0,1:T(8,128)S(1)}, u32[]{:S(2)}) copy-start(f32[2624,152]{0,1:T(8,128)S(1)} %fusion.66) | copy-start | bytes 4786180 | tf_op jit(solution)/shard_map/while
  130.6 0.8 copy-start.4
  132.3 0.6 copy-start.5
  153.7 4.0 %copy-start.1 = (f32[2624,152]{0,1:T(8,128)S(1)}, f32[2624,152]{0,1:T(8,128)}, u32[]{:S(2)}) copy-start(f32[2624,152]{0,1:T(8,128)} %get-tuple-element.430) | copy-start | bytes 4786180 | tf_op jit(solution)/shard_map/while
  162.2 14.9 %copy-start.2 = (f32[2624,152]{0,1:T(8,128)}, f32[2624,152]{0,1:T(8,128)S(1)}, u32[]{:S(2)}) copy-start(f32[2624,152]{0,1:T(8,128)S(1)} %fusion.66) | copy-start | bytes 4786180 | tf_op jit(solution)/shard_map/while
  185.2 0.8 copy-start.4
  186.9 0.6 copy-start.5
  208.3 4.0 %copy-start.1 = (f32[2624,152]{0,1:T(8,128)S(1)}, f32[2624,152]{0,1:T(8,128)}, u32[]{:S(2)}) copy-start(f32[2624,152]{0,1:T(8,128)} %get-tuple-element.430) | copy-start | bytes 4786180 | tf_op jit(solution)/shard_map/while
  216.8 14.9 %copy-start.2 = (f32[2624,152]{0,1:T(8,128)}, f32[2624,152]{0,1:T(8,128)S(1)}, u32[]{:S(2)}) copy-start(f32[2624,152]{0,1:T(8,128)S(1)} %fusion.66) | copy-start | bytes 4786180 | tf_op jit(solution)/shard_map/while
  239.8 0.8 copy-start.4
  241.5 0.6 copy-start.5
  262.9 4.0 %copy-start.1 = (f32[2624,152]{0,1:T(8,128)S(1)}, f32[2624,152]{0,1:T(8,128)}, u32[]{:S(2)}) copy-start(f32[2624,152]{0,1:T(8,128)} %get-tuple-element.430) | copy-start | bytes 4786180 | tf_op jit(solution)/shard_map/while
  271.4 14.9 %copy-start.2 = (f32[2624,152]{0,1:T(8,128)}, f32[2624,152]{0,1:T(8,128)S(1)}, u32[]{:S(2)}) copy-start(f32[2624,152]{0,1:T(8,128)S(1)} %fusion.66) | copy-start | bytes 4786180 | tf_op jit(solution)/shard_map/while
  294.4 0.8 copy-start.4
  296.1 0.6 copy-start.5
  302.1 25.7 %all-to-all-start.1 = ((bf16[128,2,1520]{2,1,0:T(2,128)(2,1)}), bf16[128,2,1520]{2,1,0:T(2,128)(2,1)S(1)}, u32[]{:S(2)}, u32[]{:S(2)}) async-start(bf16[128,2,1520]{2,1,0:T(2,128)(2,1)} %reshape.208), calls=%async_computation.1 | async-start | bytes 1572864 | tf_op jit(solution)/shard_map/all_to_all | solution.py:114
  330.0 17.2 %copy-start.6 = (f32[64,152]{1,0:T(8,128)S(1)}, f32[64,152]{1,0:T(8,128)}, u32[]{:S(2)}) copy-start(f32[64,152]{1,0:T(8,128)} %get-tuple-element.279) | copy-start | bytes 116740
  330.0 17.2 %copy-start.9 = (f32[152,152]{1,0:T(8,128)S(1)}, f32[152,152]{1,0:T(8,128)}, u32[]{:S(2)}) copy-start(f32[152,152]{1,0:T(8,128)} %param.18) | copy-start | bytes 277252
  330.1 17.2 %copy-start.11 = (bf16[64,152]{1,0:T(8,128)(2,1)S(1)}, bf16[64,152]{1,0:T(8,128)(2,1)}, u32[]{:S(2)}) copy-start(bf16[64,152]{1,0:T(8,128)(2,1)} %param.15) | copy-start | bytes 58372
  348.3 9.0 %copy-start.8 = (bf16[64,152]{1,0:T(8,128)(2,1)}, bf16[64,152]{1,0:T(8,128)(2,1)S(1)}, u32[]{:S(2)}) copy-start(bf16[64,152]{1,0:T(8,128)(2,1)S(1)} %fusion.17) | copy-start | bytes 58372
  348.3 8.7 %collective-permute-start.1 = (bf16[38,152]{1,0:T(8,128)(2,1)S(1)}, bf16[38,152]{1,0:T(8,128)(2,1)S(1)}, u32[]{:S(2)}, u32[]{:S(2)}) collective-permute-start(bf16[38,152]{1,0:T(8,128)(2,1)S(1)} %slice.68), channel_id=1, source_target_pairs={{0,1},{1,2},{2,3},{3,4},{4,5},{5,6},{6,7},{7,8},{8,9},{9,10},{10,1... | collective-permute-start | bytes 34664 | tf_op jit(solution)/shard_map/ppermute | solution.py:14
where the time goes:
time: 361 us; the launch traced here: 358 us
  local copies, waits for them, and re-layouts  201 us (56%)
  matrix products  87.5 us (24%)
  starting transfers between devices  27.8 us (8%)
  waiting for transfers between devices  21.2 us (6%)
  other arithmetic  19.5 us (5%)
    gather x4, local copies, waits for them, and re-layouts, block_step(): m2l[ids]  59.6 us
    gather x4, local copies, waits for them, and re-layouts, block_step(): m2l[NOPS - 1 - ids]  57.3 us
    unnamed x30, local copies, waits for them, and re-layouts  48.1 us
    dot_general x12, matrix products, contract_rows(): lax.dot_general(picker, values, (((0,), (0,)), ((), ())), precision=preci...  36.9 us
    dot_general x4, matrix products, block_step(): jnp.dot(pick_table, table_rows, preferred_element_type=jnp.float32)  15.6 us
    scatter-add x1, other arithmetic, shards(): jax.ops.segment_sum(came_back.reshape(devices * CAP, width_dens), owner_r...  15.3 us
    dot_general x4, matrix products, block_step(): jnp.einsum('kcj,kji->kci', owner_dens.reshape(per_block, OPCAP, width_den...  15 us
    dot_general x4, matrix products, block_step(): jnp.einsum('kcj,kji->kci', partner_dens.reshape(per_block, OPCAP, width_d...  15 us
  transfers between devices with their start and end apart: 4, of which 3 were waited for; matrix products, arithmetic and copies ran while one was open for 12% of the time, Pallas kernels for 0%

commit v1 on v0

v1 whole, which is shorter than its diff:
```python
import functools

import jax
import jax.numpy as jnp
import numpy as np
from jax import lax
from jax.experimental import pallas as pl
from jax.experimental.pallas import tpu as pltpu
from jax.sharding import PartitionSpec as P
f32=jnp.float32; bf16=jnp.bfloat16
NOPS=316; CAP=20; LEAD=300; OPCAP=13
RUNS=320; SLOTS=4160; COLS=4224; GROUP=8
def pack_maps():
    row=np.arange(192)[:,None]; col=np.arange(160)[None,:]
    same=row//24==col//20
    main=same&(row%24==col%20)
    tail=same&(row%24==20+col%20//5)
    lane=np.arange(128)
    mask=(lane[None,:]//24==np.arange(160)[:,None]%5)
    fold=(lane[:,None]%24==lane[None,:])&(lane[:,None]<120)&(lane[None,:]<24)
    return main,tail,mask,fold
def translate_runs(ids,src,table,t_ref,xs,ymain,ytail):
    def group(g,_):
        for u in range(GROUP):
            r=g*GROUP+u
            k=ids[r]
            for c in range(OPCAP):
                i=pl.multiple_of(src[r*OPCAP+c],2)
                xs[u,2*c:2*c+2,:]=table[pl.ds(i,2),:]
            main=xs[u,pl.ds(0,16,stride=2),:]
            tail=xs[u,pl.ds(1,16,stride=2),:]
            x=jnp.concatenate([main,tail[:,:24]],axis=1).astype(bf16)
            y=jnp.dot(x,t_ref[k],preferred_element_type=f32)
            base=g*(GROUP*OPCAP)+u*OPCAP
            ymain[pl.ds(base,16),:]=y[:,:128]
            ytail[pl.ds(base,16),0:24]=y[:,128:]
        return 0
    lax.fori_loop(0,RUNS//GROUP,group,0)
def store_rows(table,first,main,tail):
    n=main.shape[0]
    table[pl.ds(first,n,stride=2),:]=main
    table[pl.ds(first+1,n,stride=2),:]=tail
def widen(rows):
    up=rows.astype(f32)
    return up[:,:128],jnp.concatenate([up[:,128:],jnp.zeros((up.shape[0],104),f32)],axis=1)
def backward_kernel(ids,src,up_ref,partner_ref,pm_ref,pt_ref,mask_ref,rep_ref,t_ref,local_ref,out_ref,t_out,table,xs,ymain,ytail,yb):
    xs[...]=jnp.zeros_like(xs)
    ymain[4096:,:]=jnp.zeros((ymain.shape[0]-4096,128),f32)
    ytail[...]=jnp.zeros_like(ytail)
    m,t=widen(up_ref[...])
    store_rows(table,0,m,t)
    translate_runs(ids,src,table,t_ref,xs,ymain,ytail)
    def conv(i,_):
        s=pl.ds(pl.multiple_of(i*128,128),128)
        yb[s,0:128]=ymain[s,:].astype(bf16)
        yb[s,128:256]=ytail[s,:].astype(bf16)
        return 0
    lax.fori_loop(0,COLS//128,conv,0,unroll=3)
    partner=partner_ref[...]
    def sums(first,n):
        rows=lax.broadcasted_iota(jnp.int32,(n,COLS),0)+first
        hot=jnp.where(rows==partner,1.0,0.0).astype(bf16)
        return jnp.dot(hot,yb[...],preferred_element_type=f32)
    own=sums(0,64)
    local_ref[...]=own[:,:152]
    def step(g,_):
        a=sums(64+320*g,320)
        for h in range(2):
            part=a[160*h:160*h+160]
            main=part[:,:128].astype(bf16)
            tail=(jnp.dot(part[:,128:].astype(bf16),rep_ref[...],preferred_element_type=f32)*mask_ref[...]).astype(bf16)
            packed=jnp.dot(pm_ref[...],main,preferred_element_type=f32)+jnp.dot(pt_ref[...],tail,preferred_element_type=f32)
            out_ref[pl.ds(pl.multiple_of(384*g+192*h,192),192),:]=packed.astype(bf16)
        return 0
    lax.fori_loop(0,8,step,0)
def forward_kernel(ids,src,up_ref,came_ref,box_ref,pm_ref,pt_ref,mask_ref,fold_ref,t_ref,own_ref,table,xs,ymain,ytail,yb):
    xs[...]=jnp.zeros_like(xs)
    ymain[4096:,:]=jnp.zeros((ymain.shape[0]-4096,128),f32)
    ytail[...]=jnp.zeros_like(ytail)
    m,t=widen(up_ref[...])
    store_rows(table,0,m,t)
    table[5248:5264,:]=jnp.zeros((16,128),f32)
    def unpack(g,_):
        rows=came_ref[pl.ds(pl.multiple_of(192*g,192),192),:]
        main=jnp.dot(pm_ref[...],rows,preferred_element_type=f32)
        tail=(jnp.dot(pt_ref[...],rows,preferred_element_type=f32)*mask_ref[...]).astype(bf16)
        tail=jnp.dot(tail,fold_ref[...],preferred_element_type=f32)
        store_rows(table,128+320*g,main,tail)
        return 0
    lax.fori_loop(0,16,unpack,0,unroll=2)
    translate_runs(ids,src,table,t_ref,xs,ymain,ytail)
    def conv(i,_):
        s=pl.ds(pl.multiple_of(i*128,128),128)
        yb[s,0:128]=ymain[s,:].astype(bf16)
        yb[s,128:256]=ytail[s,:].astype(bf16)
        return 0
    lax.fori_loop(0,COLS//128,conv,0,unroll=3)
    rows=lax.broadcasted_iota(jnp.int32,(64,COLS),0)
    hot=jnp.where(rows==box_ref[...],1.0,0.0).astype(bf16)
    own_ref[...]=jnp.dot(hot,yb[...],preferred_element_type=f32)[:,:152]
SM=pl.BlockSpec(memory_space=pltpu.SMEM); VM=pl.BlockSpec(memory_space=pltpu.VMEM)
def scratch(rows):
    return [pltpu.VMEM((rows,128),f32),pltpu.VMEM((GROUP,32,128),f32),pltpu.VMEM((COLS,128),f32),pltpu.VMEM((COLS,128),f32),pltpu.VMEM((COLS,256),bf16)]
LIM=16*1024*1024
def backward(ids,src,up,partner_row,t):
    main,tail,mask,fold=pack_maps()
    c=lambda a,d: jnp.asarray(a.astype(np.float32),d)
    return pl.pallas_call(backward_kernel,in_specs=[SM,SM]+[VM]*7,out_specs=[VM,VM,VM],input_output_aliases={8:2},
        out_shape=[jax.ShapeDtypeStruct((64,152),f32),jax.ShapeDtypeStruct((3072,128),bf16),pltpu.VMEM((NOPS,152,152),bf16)],
        scratch_shapes=scratch(128),compiler_params=pltpu.CompilerParams(vmem_limit_bytes=LIM),name="backward")(
        ids,src,up,partner_row,c(main,bf16),c(tail,bf16),c(mask,f32),c(fold.T,bf16),t)
def forward(ids,src,up,came,box_row,t):
    main,tail,mask,fold=pack_maps()
    c=lambda a,d: jnp.asarray(a.astype(np.float32),d)
    return pl.pallas_call(forward_kernel,in_specs=[SM,SM]+[VM]*8,out_specs=VM,
        out_shape=jax.ShapeDtypeStruct((64,152),f32),
        scratch_shapes=scratch(5264),compiler_params=pltpu.CompilerParams(vmem_limit_bytes=LIM),name="forward")(
        ids,src,up,came,box_row,c(main.T,bf16),c(tail.T,bf16),c(mask,f32),c(fold,bf16),t)
HALF=76
def operator_kernel(m_ref,o_ref,s1,s2):
    stride=153; first=pl.program_id(0)*128; j0=pl.program_id(1)*HALF
    def turn(j,_):
        t=m_ref[j].T.astype(f32)
        s1[pl.ds(j0+j,128,stride=stride),:]=t[:,:128]
        s2[pl.ds(j0+j,128,stride=stride),0:24]=t[:,128:]
        return 0
    lax.fori_loop(0,HALF,turn,0,unroll=4)
    @pl.when(pl.program_id(1)==1)
    def _():
        def collect(k,_):
            o_ref[first+k,:,0:128]=s1[pl.ds(k*stride,152),:].astype(bf16)
            o_ref[first+k,:,128:152]=s2[pl.ds(k*stride,152),:][:,:24].astype(bf16)
            return 0
        lax.fori_loop(0,jnp.minimum(128,NOPS-first),collect,0)
def operators(m):
    t=pl.pallas_call(operator_kernel,grid=(3,2),in_specs=[pl.BlockSpec((HALF,152,128),lambda i,j:(j,0,i))],
      out_specs=VM,out_shape=pltpu.VMEM((NOPS,152,152),bf16),
      scratch_shapes=[pltpu.VMEM((128*153,128),f32)]*2,
      compiler_params=pltpu.CompilerParams(vmem_limit_bytes=27*1024*1024),name="operators")(m)
    return t

def slot_rows(send):
    flat=jnp.pad(send,((0,0),(0,4)),constant_values=-1).reshape(1,3072)
    parts=[flat]
    split=send.reshape(128,4,5)
    for t in range(5):
        parts.append(jnp.pad(split[:,:,t],((0,0),(20,0)),constant_values=-1).reshape(1,3072))
    return jnp.concatenate(parts+[jnp.full((2,3072),-1,jnp.int32)])
def slot_hot(slot_ref):
    boxes=lax.broadcasted_iota(jnp.int32,(64,3072),0)
    return [jnp.where(boxes==slot_ref[b:b+1,:],1.0,0.0).astype(bf16) for b in range(6)]
def send_kernel(slot_ref,up_ref,rep_ref,out_ref):
    up=up_ref[...]
    tail=jnp.dot(jnp.concatenate([up[:,128:],jnp.zeros((64,104),bf16)],axis=1),rep_ref[...],preferred_element_type=f32)
    lane=lax.broadcasted_iota(jnp.int32,(64,128),1)
    values=[up[:,:128]]+[jnp.where((lane>=24*t)&(lane<24*t+24),tail,0.0).astype(bf16) for t in range(5)]
    hot=jnp.concatenate(slot_hot(slot_ref),axis=0)
    out_ref[...]=lax.dot_general(hot,jnp.concatenate(values,axis=0),(((0,),(0,)),((),())),preferred_element_type=f32).astype(bf16)
def pack_sends(slots,up):
    fold=pack_maps()[3]
    return pl.pallas_call(send_kernel,in_specs=[VM]*3,out_specs=VM,out_shape=jax.ShapeDtypeStruct((3072,128),bf16),
        compiler_params=pltpu.CompilerParams(vmem_limit_bytes=LIM),name="send")(slots,up,jnp.asarray(fold.T.astype(np.float32),bf16))
def finish_kernel(slot_ref,came_ref,local_ref,own_ref,c2e_ref,coarse_ref,parent_ref):
    hot=jnp.concatenate(slot_hot(slot_ref),axis=0)
    got=jnp.dot(hot,came_ref[...],preferred_element_type=f32)
    tail=got[64:128,0:24]
    for t in range(1,5):
        tail=tail+got[64+64*t:128+64*t,24*t:24*t+24]
    check=local_ref[...]+own_ref[...]+jnp.concatenate([got[:64],tail],axis=1)
    parent=jnp.dot(check,c2e_ref[...],precision=lax.Precision.HIGHEST,preferred_element_type=f32)+coarse_ref[...].astype(f32)
    parent_ref[...]=parent.astype(bf16)
def finish(slots,came,local,own,c2e,coarse):
    return pl.pallas_call(finish_kernel,in_specs=[VM]*6,out_specs=VM,out_shape=jax.ShapeDtypeStruct((64,152),bf16),
        compiler_params=pltpu.CompilerParams(vmem_limit_bytes=LIM),name="finish")(slots,came,local,own,c2e,coarse)
def pad_to(a,n,v):
    return jnp.concatenate([a,jnp.full((n-a.shape[0],),v,a.dtype)])
AXES=("slab","sub")
def shifted(x, by):
    count = lax.axis_size(AXES)
    return lax.ppermute(x, AXES, [(i, (i + by) % count) for i in range(count)])
def exchange(x):
    return lax.all_to_all(x.reshape(128,24,128),AXES,split_axis=0,concat_axis=0,tiled=True).reshape(3072,128)
def shards(leaves, coarse_local, m2m, m2l, c2e, l2l, send_box, pair_box, pair_partner, pair_op):
    width=152; box_count=64; edge=38
    front=jnp.concatenate([jnp.zeros((8*edge-LEAD,width),bf16),leaves[:LEAD]])
    front_sum=jnp.einsum("poj,oji->pi",front.reshape(edge,8,width),m2m,preferred_element_type=f32)
    arrived=shifted(front_sum,-1)
    ops=operators(jnp.transpose(m2l,(1,2,0)))
    own_rows=jnp.concatenate([leaves[LEAD:],jnp.zeros((LEAD,width),bf16)])
    up_sum=jnp.einsum("poj,oji->pi",own_rows.reshape(box_count,8,width),m2m,preferred_element_type=f32)
    up=up_sum.at[box_count-edge:].add(arrived).astype(bf16)
    slots=slot_rows(send_box.reshape(128,CAP))
    ids=pair_op.reshape(NOPS,OPCAP)[:,0]
    ids_f=pad_to(ids,RUNS,0); ids_b=pad_to(NOPS-1-ids,RUNS,0)
    src_f=pad_to(2*jnp.where(pair_partner>=0,pair_partner,2624),SLOTS,2*2624)
    src_b=pad_to(2*pair_box,SLOTS,0)
    partner_row=pad_to(pair_partner,COLS,-1)[None]
    box_row=pad_to(pair_box,COLS,-1)[None]
    came=exchange(pack_sends(slots,up))
    ops=pltpu.with_memory_space_constraint(ops,pltpu.VMEM)
    local,to_owners,ops=backward(ids_b,src_b,up,partner_row,ops)
    returned=exchange(to_owners)
    ops=pltpu.with_memory_space_constraint(ops,pltpu.VMEM)
    own=forward(ids_f,src_f,up,came,box_row,ops)
    parent=finish(slots,returned,local,own,c2e,coarse_local)
    earlier=shifted(parent[box_count-edge:],1)
    head=jnp.einsum("pj,oji->poi",earlier,l2l,preferred_element_type=f32).reshape(8*edge,width)
    own_part=jnp.einsum("pj,oji->poi",parent,l2l,preferred_element_type=f32).reshape(8*box_count,width)
    leaf_local=jnp.concatenate([head[8*edge-LEAD:],own_part[:8*box_count-LEAD]])
    return (parent,leaf_local)


def solution(mesh):
    split = P(("slab", "sub"), None)
    flat = P(("slab", "sub"))
    return jax.shard_map(
        shards,
        mesh=mesh,
        in_specs=(split, split, P(), P(), P(), P(), split, flat, flat, flat),
        out_specs=(split, split),
        check_vma=False,
    )
```

time: 361 us -> 146 us (0.40)
  local copies, waits for them, and re-layouts: 201 us -> 42.9 us
  matrix products: 87.5 us -> 3.9 us
  Pallas kernels: 0 us -> 65.2 us
  other arithmetic: 19.5 us -> 1.54 us
  waiting for transfers between devices: 21.2 us -> 6.33 us
  starting transfers between devices: 27.8 us -> 23.6 us
    gather x10 -> x0, local copies, waits for them, and re-layouts: 126 us -> none  [the longest x4 59.6 us: block_step(): m2l[ids]]
    dot_general x33 -> x4, matrix products: 87.5 us -> 3.9 us  [the longest x1 1.34 us: shards(): jnp.einsum('poj,oji->pi', own_rows.reshape(box_count, 8, width), m2m, pre...]
    pallas_call x0 -> x5, Pallas kernels: none -> 65.2 us  [the longest x1 25.2 us: backward(): pl.pallas_call(backward_kernel, in_specs=[SM, SM] + [VM] * 7, out_specs=[...]
    scatter-add x1 -> x0, other arithmetic: 15.3 us -> none  [shards(): jax.ops.segment_sum(came_back.reshape(devices * CAP, width_dens), owner_r...]
    unnamed x30 -> x42, local copies, waits for them, and re-layouts: 48.1 us -> 34.8 us
    all_to_all x2, waiting for transfers between devices: 12.8 us -> 0.01 us  [exchange(): lax.all_to_all(x.reshape(128, 24, 128), AXES, split_axis=0, concat_axis=0...]
    while x33 -> x0, local copies, waits for them, and re-layouts: 8.41 us -> none
    dynamic_slice x8 -> x0, local copies, waits for them, and re-layouts: 6.26 us -> none  [the longest x4 3.15 us: block_step(): sources = lax.dynamic_slice_in_dim(source_rows, first, block_rows)]
  transfers between devices with their start and end apart: 4 -> 4, of which waited for: 3 -> 1; matrix products, arithmetic and copies ran while one was open for 12% -> 7% of each run, Pallas kernels for 0% -> 43%
where the time goes in v1:
time: 146 us; the launch traced here: 145 us
  Pallas kernels  65.2 us (45%)
  local copies, waits for them, and re-layouts  42.9 us (29%)
  starting transfers between devices  23.6 us (16%)
  waiting for transfers between devices  6.33 us (4%)
  matrix products  3.9 us (3%)
  other arithmetic  1.54 us (1%)
    unnamed x42, local copies, waits for them, and re-layouts  34.8 us
    pallas_call x1, Pallas kernels, backward(): pl.pallas_call(backward_kernel, in_specs=[SM, SM] + [VM] * 7, out_specs=[...  25.2 us
    pallas_call x1, Pallas kernels, operators(): pl.pallas_call(operator_kernel, grid=(3, 2), in_specs=[pl.BlockSpec((HALF...  20.9 us
    pallas_call x1, Pallas kernels, forward(): pl.pallas_call(forward_kernel, in_specs=[SM, SM] + [VM] * 8, out_specs=VM...  15.5 us
    all_to_all x2, starting transfers between devices, exchange(): lax.all_to_all(x.reshape(128, 24, 128), AXES, split_axis=0, concat_axis=0...  14.4 us
    ppermute x2, starting transfers between devices, shifted(): return lax.ppermute(x, AXES, [(i, (i + by) % count) for i in range(count)])  9.25 us
    ppermute x2, waiting for transfers between devices, shifted(): return lax.ppermute(x, AXES, [(i, (i + by) % count) for i in range(count)])  6.32 us
  transfers between devices with their start and end apart: 4, of which 1 were waited for; matrix products, arithmetic and copies ran while one was open for 7% of the time, Pallas kernels for 43%

profile of v1, /device:TPU:0, one launch (start us, length us, event | category | flops | bytes accessed | tf_op | source)
XLA Modules:
  0.0 144.7 jit_solution(2707354556631301623)
XLA Ops:
  0.6 1.0 slice.60
  1.6 0.1 copy.52
  1.8 1.3 convolution_bitcast_fusion.1
  3.2 8.3 %collective-permute-start = (f32[38,152]{1,0:T(8,128)S(1)}, f32[38,152]{1,0:T(8,128)S(1)}, u32[]{:S(2)}, u32[]{:S(2)}) collective-permute-start(f32[38,152]{1,0:T(8,128)S(1)} %convolution_bitcast_fusion.1), channel_id=1, source_target_pairs={{0,127},{1,0},{2,1},{3,2},{4,3},{5,4},{6,5},{7,6},{8,7},{9,8},{10,... | collective-permute-start | bytes 69320 | tf_op jit(solution)/shard_map/ppermute | solution.py:180
  11.4 1.0 slice.58
  12.4 0.7 reduce.2
  13.1 0.3 reshape_reshape.3
  13.5 0.6 fusion.7
  14.1 0.1 copy.51
  14.2 1.3 convolution_bitcast_fusion
  15.6 0.1 reshape.78
  15.8 0.1 reshape.79
  16.0 0.1 copy.53
  16.2 0.1 reshape.80
  16.4 0.1 copy.54
  16.6 0.1 reshape.81
  16.9 0.1 copy.55
  17.1 0.1 reshape.82
  17.3 0.1 copy.56
  17.5 0.1 reshape.83
  17.7 0.1 copy.57
  18.0 0.1 reshape.84
  18.1 0.1 concatenate.32.slot_ref
  18.3 0.3 scatter-add.4
  18.6 0.7 copy-done.7
  19.3 1.9 %send.1 = bf16[3072,128]{1,0:T(8,128)(2,1)} custom-call(s32[8,3072]{1,0:T(8,128)S(1)} %concatenate.32.slot_ref, bf16[64,152]{1,0:T(8,128)(2,1)S(1)} %convert_element_type.3.up_ref, bf16[128,128]{1,0:T(8,128)(2,1)S(1)} %copy-done.7), custom_call_target="tpu_custom_call" | custom-call | tf_op jit(solution)/shard_map/send/pallas_call | solution.py:161
  21.2 4.6 %all-to-all-start.1 = ((bf16[128,24,128]{2,1,0:T(8,128)(2,1)}), bf16[128,24,128]{2,1,0:T(8,128)(2,1)S(1)}, u32[]{:S(2)}, u32[]{:S(2)}) async-start(bf16[128,24,128]{2,1,0:T(8,128)(2,1)} %bitcast.12), calls=%async_computation.1 | async-start | bytes 1572864 | tf_op jit(solution)/shard_map/all_to_all | solution.py:182
  25.9 0.9 reshape.85
  26.8 0.1 slice_reduce_fusion
  27.0 0.7 broadcast_multiply_fusion
  27.7 0.7 concatenate.37
  28.5 20.9 %operators.1.t_ref = bf16[316,152,152]{2,1,0:T(8,128)(2,1)S(1)} custom-call(bf16[152,152,316]{2,1,0:T(8,128)(2,1)} %bitcast.36), custom_call_target="tpu_custom_call" | custom-call | tf_op jit(solution)/shard_map/operators/pallas_call | solution.py:136
  49.4 8.1 %copy-done.1 = bf16[316,152,152]{2,1,0:T(8,128)(2,1)} copy-done((bf16[316,152,152]{2,1,0:T(8,128)(2,1)}, bf16[316,152,152]{2,1,0:T(8,128)(2,1)S(1)}, u32[]{:S(2)}) %copy-start.1) | copy-done | bytes 14601752
  57.5 8.0 %copy-done.2 = bf16[316,152,152]{2,1,0:T(8,128)(2,1)S(1)} copy-done((bf16[316,152,152]{2,1,0:T(8,128)(2,1)S(1)}, bf16[316,152,152]{2,1,0:T(8,128)(2,1)}, u32[]{:S(2)}) %copy-start.2) | copy-done | bytes 14601752
  65.5 25.2 %backward.1 = (f32[64,152]{1,0:T(8,128)S(1)}, bf16[3072,128]{1,0:T(8,128)(2,1)}, bf16[316,152,152]{2,1,0:T(8,128)(2,1)S(1)}) custom-call(s32[320]{0:T(512)S(1)} %concatenate.33.ids, s32[4160]{0:T(1024)S(1)} %concatenate.34.src, bf16[64,152]{1,0:T(8,128)(2,1)S(1)} %convert_element_type.3.up_ref, ...), custom_call_target="tpu_custom_call", output_to_operand_aliasing={{2}: (8, {})} | custom-call | tf_op jit(solution)/shard_map/backward/pallas_call | solution.py:108
  90.7 8.1 %copy-done.3 = bf16[316,152,152]{2,1,0:T(8,128)(2,1)} copy-done((bf16[316,152,152]{2,1,0:T(8,128)(2,1)}, bf16[316,152,152]{2,1,0:T(8,128)(2,1)S(1)}, u32[]{:S(2)}) %copy-start.3) | copy-done | bytes 14601752
  98.8 9.8 %all-to-all-start = ((bf16[128,24,128]{2,1,0:T(8,128)(2,1)}), bf16[128,24,128]{2,1,0:T(8,128)(2,1)S(1)}, u32[]{:S(2)}, u32[]{:S(2)}) async-start(bf16[128,24,128]{2,1,0:T(8,128)(2,1)} %bitcast.10), calls=%async_computation | async-start | bytes 1572864 | tf_op jit(solution)/shard_map/all_to_all | solution.py:182
  108.7 8.0 %copy-done.4 = bf16[316,152,152]{2,1,0:T(8,128)(2,1)S(1)} copy-done((bf16[316,152,152]{2,1,0:T(8,128)(2,1)S(1)}, bf16[316,152,152]{2,1,0:T(8,128)(2,1)}, u32[]{:S(2)}) %copy-start.4) | copy-done | bytes 14601752
  116.7 15.5 %forward.1.own_ref = f32[64,152]{1,0:T(8,128)S(1)} custom-call(s32[320]{0:T(512)S(1)} %concatenate.38.ids, s32[4160]{0:T(1024)S(1)} %concatenate.39.src, bf16[64,152]{1,0:T(8,128)(2,1)S(1)} %convert_element_type.3.up_ref, bf16[3072,128]{1,0:T(8,128)(2,1)S(1)} %bitcast.34, s32[1,4224]{1,0:T(1,128)S(1)} %broadcast_in_dim.20.box_ref, ...), custom_call_target="tpu_custom_call" | custom-call | tf_op jit(solution)/shard_map/forward/pallas_call | solution.py:115
  132.2 1.8 %finish.1 = bf16[64,152]{1,0:T(8,128)(2,1)} custom-call(s32[8,3072]{1,0:T(8,128)S(1)} %concatenate.32.slot_ref, bf16[3072,128]{1,0:T(8,128)(2,1)S(1)} %bitcast.35, f32[64,152]{1,0:T(8,128)S(1)} %get-tuple-element.18.local_ref, f32[64,152]{1,0:T(8,128)S(1)} %forward.1.own_ref, f32[152,152]{1,0:T(8,128)S(1)} %copy-done.6, bf16[64,152]{1,0:T(8,128)(2,1)S(1)} %copy-done.14), custom_call_target="tpu_custom_call" | custom-call | tf_op jit(solution)/shard_map/finish/pallas_call | solution.py:173
  134.0 0.7 slice.71
  134.7 1.0 collective-permute-start.1
  135.7 1.0 fusion.2
  136.7 0.3 copy.64
  137.0 6.3 %collective-permute-done.1 = bf16[38,152]{1,0:T(8,128)(2,1)S(1)} collective-permute-done((bf16[38,152]{1,0:T(8,128)(2,1)S(1)}, bf16[38,152]{1,0:T(8,128)(2,1)S(1)}, u32[]{:S(2)}, u32[]{:S(2)}) %collective-permute-start.1) | collective-permute-done | bytes 11584 | tf_op jit(solution)/shard_map/ppermute | solution.py:180
  143.4 0.2 fusion.5
  143.6 0.1 copy.65
  143.8 0.9 copy.50
  (60 shorter events, 1.2 us)
Async XLA Ops:
  0.6 135.1 %copy-start = (bf16[8,152,152]{2,1,0:T(8,128)(2,1)S(1)}, bf16[8,152,152]{2,1,0:T(8,128)(2,1)}, u32[]{:S(2)}) copy-start(bf16[8,152,152]{2,1,0:T(8,128)(2,1)} %param.26) | copy-start | bytes 1108996
  3.2 15.1 %collective-permute-start = (f32[38,152]{1,0:T(8,128)S(1)}, f32[38,152]{1,0:T(8,128)S(1)}, u32[]{:S(2)}, u32[]{:S(2)}) collective-permute-start(f32[38,152]{1,0:T(8,128)S(1)} %convolution_bitcast_fusion.1), channel_id=1, source_target_pairs={{0,127},{1,0},{2,1},{3,2},{4,3},{5,4},{6,5},{7,6},{8,7},{9,8},{10,... | collective-permute-start | bytes 69320 | tf_op jit(solution)/shard_map/ppermute | solution.py:180
  15.6 41.9 %copy-start.5 = (f32[160,128]{1,0:T(8,128)S(1)}, f32[160,128]{1,0:T(8,128)}, u32[]{:S(2)}) copy-start(f32[160,128]{1,0:T(8,128)} %constant.64.clone.mask_ref) | copy-start | bytes 245764
  15.6 41.9 %copy-start.8 = (bf16[128,128]{1,0:T(8,128)(2,1)S(1)}, bf16[128,128]{1,0:T(8,128)(2,1)}, u32[]{:S(2)}) copy-start(bf16[128,128]{1,0:T(8,128)(2,1)} %constant.61.clone.rep_ref) | copy-start | bytes 98308
  15.6 41.9 %copy-start.9 = (bf16[192,160]{1,0:T(8,128)(2,1)S(1)}, bf16[192,160]{1,0:T(8,128)(2,1)}, u32[]{:S(2)}) copy-start(bf16[192,160]{1,0:T(8,128)(2,1)} %constant.62.clone.pm_ref) | copy-start | bytes 184324
  15.6 41.9 %copy-start.10 = (bf16[192,160]{1,0:T(8,128)(2,1)S(1)}, bf16[192,160]{1,0:T(8,128)(2,1)}, u32[]{:S(2)}) copy-start(bf16[192,160]{1,0:T(8,128)(2,1)} %constant.63.clone.pt_ref) | copy-start | bytes 184324
  18.6 0.8 copy-start.7
  21.2 77.6 %all-to-all-start.1 = ((bf16[128,24,128]{2,1,0:T(8,128)(2,1)}), bf16[128,24,128]{2,1,0:T(8,128)(2,1)S(1)}, u32[]{:S(2)}, u32[]{:S(2)}) async-start(bf16[128,24,128]{2,1,0:T(8,128)(2,1)} %bitcast.12), calls=%async_computation.1 | async-start | bytes 1572864 | tf_op jit(solution)/shard_map/all_to_all | solution.py:182
  28.4 80.1 %copy-start.15 = (s32[4108]{0:T(1024)S(1)}, s32[4108]{0:T(1024)}, u32[]{:S(2)}) copy-start(s32[4108]{0:T(1024)} %param.28) | copy-start | bytes 49300
  28.5 80.2 %copy-start.16 = (s32[4108]{0:T(1024)S(1)}, s32[4108]{0:T(1024)}, u32[]{:S(2)}) copy-start(s32[4108]{0:T(1024)} %param.29) | copy-start | bytes 49300
  28.5 80.2 %copy-start.11 = (bf16[160,192]{1,0:T(8,128)(2,1)S(1)}, bf16[160,192]{1,0:T(8,128)(2,1)}, u32[]{:S(2)}) copy-start(bf16[160,192]{1,0:T(8,128)(2,1)} %constant.65.clone.pm_ref) | copy-start | bytes 184324
  28.5 80.2 %copy-start.12 = (bf16[160,192]{1,0:T(8,128)(2,1)S(1)}, bf16[160,192]{1,0:T(8,128)(2,1)}, u32[]{:S(2)}) copy-start(bf16[160,192]{1,0:T(8,128)(2,1)} %constant.66.clone.pt_ref) | copy-start | bytes 184324
  28.5 80.2 %copy-start.13 = (bf16[128,128]{1,0:T(8,128)(2,1)S(1)}, bf16[128,128]{1,0:T(8,128)(2,1)}, u32[]{:S(2)}) copy-start(bf16[128,128]{1,0:T(8,128)(2,1)} %constant.67.clone.fold_ref) | copy-start | bytes 98308
  49.4 8.1 %copy-start.1 = (bf16[316,152,152]{2,1,0:T(8,128)(2,1)}, bf16[316,152,152]{2,1,0:T(8,128)(2,1)S(1)}, u32[]{:S(2)}) copy-start(bf16[316,152,152]{2,1,0:T(8,128)(2,1)S(1)} %operators.1.t_ref) | copy-start | bytes 43805188
  57.5 8.0 %copy-start.2 = (bf16[316,152,152]{2,1,0:T(8,128)(2,1)S(1)}, bf16[316,152,152]{2,1,0:T(8,128)(2,1)}, u32[]{:S(2)}) copy-start(bf16[316,152,152]{2,1,0:T(8,128)(2,1)} %copy-done.1) | copy-start | bytes 43805188
  65.5 66.7 %copy-start.6 = (f32[152,152]{1,0:T(8,128)S(1)}, f32[152,152]{1,0:T(8,128)}, u32[]{:S(2)}) copy-start(f32[152,152]{1,0:T(8,128)} %c2e_ref.1) | copy-start | bytes 277252
  65.5 66.7 %copy-start.14 = (bf16[64,152]{1,0:T(8,128)(2,1)S(1)}, bf16[64,152]{1,0:T(8,128)(2,1)}, u32[]{:S(2)}) copy-start(bf16[64,152]{1,0:T(8,128)(2,1)} %coarse_ref.1) | copy-start | bytes 58372
  90.7 8.1 %copy-start.3 = (bf16[316,152,152]{2,1,0:T(8,128)(2,1)}, bf16[316,152,152]{2,1,0:T(8,128)(2,1)S(1)}, u32[]{:S(2)}) copy-start(bf16[316,152,152]{2,1,0:T(8,128)(2,1)S(1)} %get-tuple-element.19.t_ref) | copy-start | bytes 43805188
  98.8 33.4 %all-to-all-start = ((bf16[128,24,128]{2,1,0:T(8,128)(2,1)}), bf16[128,24,128]{2,1,0:T(8,128)(2,1)S(1)}, u32[]{:S(2)}, u32[]{:S(2)}) async-start(bf16[128,24,128]{2,1,0:T(8,128)(2,1)} %bitcast.10), calls=%async_computation | async-start | bytes 1572864 | tf_op jit(solution)/shard_map/all_to_all | solution.py:182
  108.7 8.0 %copy-start.4 = (bf16[316,152,152]{2,1,0:T(8,128)(2,1)S(1)}, bf16[316,152,152]{2,1,0:T(8,128)(2,1)}, u32[]{:S(2)}) copy-start(bf16[316,152,152]{2,1,0:T(8,128)(2,1)} %copy-done.3) | copy-start | bytes 43805188
  134.7 8.6 %collective-permute-start.1 = (bf16[38,152]{1,0:T(8,128)(2,1)S(1)}, bf16[38,152]{1,0:T(8,128)(2,1)S(1)}, u32[]{:S(2)}, u32[]{:S(2)}) collective-permute-start(bf16[38,152]{1,0:T(8,128)(2,1)S(1)} %slice.71), channel_id=1, source_target_pairs={{0,1},{1,2},{2,3},{3,4},{4,5},{5,6},{6,7},{7,8},{8,9},{9,10},{10,1... | collective-permute-start | bytes 34664 | tf_op jit(solution)/shard_map/ppermute | solution.py:180

commit v2 on v1

v2 whole, which is shorter than its diff:
```python
import functools

import jax
import jax.numpy as jnp
import numpy as np
from jax import lax
from jax.experimental import pallas as pl
from jax.experimental.pallas import tpu as pltpu
from jax.sharding import PartitionSpec as P
f32=jnp.float32; bf16=jnp.bfloat16
NOPS=316; CAP=20; LEAD=300; OPCAP=13
RUNS=320; SLOTS=4160; COLS=4224; GROUP=32
def pack_maps():
    row=np.arange(192)[:,None]; col=np.arange(160)[None,:]
    same=row//24==col//20
    main=same&(row%24==col%20)
    tail=same&(row%24==20+col%20//5)
    lane=np.arange(128)
    mask=(lane[None,:]//24==np.arange(160)[:,None]%5)
    fold=(lane[:,None]%24==lane[None,:])&(lane[:,None]<120)&(lane[None,:]<24)
    return main,tail,mask,fold
NACC=4
CHUNK=64
def fetch_operators(t_ref,t_buf,sems):
    copies=[]
    for q in range(5):
        n=min(CHUNK,NOPS-q*CHUNK)
        copies.append(pltpu.make_async_copy(t_ref.at[pl.ds(q*CHUNK,n)],t_buf.at[pl.ds(q*CHUNK,n)],sems.at[q]))
        copies[-1].start()
    return copies
def translate_runs(places,src,dst,flip,copies,table,t_buf,xs,ys,accs):
    def group(g,_):
        for u in range(GROUP):
            k=g*GROUP+u
            first=places[NOPS-1-k if flip else k] if u<GROUP-4 else places[jnp.where(k<NOPS,NOPS-1-k,k) if flip else k]
            for c in range(OPCAP):
                i=pl.multiple_of(src[first+c],2)
                xs[u,2*c:2*c+2,:]=table[pl.ds(i,2),:]
            main=xs[u,pl.ds(0,16,stride=2),:]
            tail=xs[u,pl.ds(1,16,stride=2),:]
            x=jnp.concatenate([main,tail[:,:24]],axis=1).astype(bf16)
            y=jnp.dot(x,t_buf[jnp.minimum(k,NOPS-1)],preferred_element_type=f32)
            ys[u,pl.ds(0,16,stride=2),:]=y[:,:128]
            ys[u,pl.ds(1,16,stride=2),0:24]=y[:,128:]
            for c in range(OPCAP):
                d=pl.multiple_of(dst[first+c],2)
                acc=accs[(u*OPCAP+c)%NACC]
                acc[pl.ds(d,2),:]=acc[pl.ds(d,2),:]+ys[u,2*c:2*c+2,:]
        return 0
    for q in range(5):
        copies[q].wait()
        lax.fori_loop(q*CHUNK//GROUP,(q+1)*CHUNK//GROUP,group,0)
def zero_fill(ref):
    n=ref.shape[0]
    def fill(i,_):
        ref[pl.ds(pl.multiple_of(i*64,64),64),:]=jnp.zeros((64,128),f32)
        return 0
    lax.fori_loop(0,n//64,fill,0,unroll=4)
def sum_rows(accs,first,n):
    main=accs[0][pl.ds(first,n,stride=2),:]
    tail=accs[0][pl.ds(first+1,n,stride=2),:]
    for acc in accs[1:]:
        main=main+acc[pl.ds(first,n,stride=2),:]
        tail=tail+acc[pl.ds(first+1,n,stride=2),:]
    lane=lax.broadcasted_iota(jnp.int32,tail.shape,1)
    return main,jnp.where(lane<24,tail,0.0)
def store_rows(table,first,main,tail):
    n=main.shape[0]
    table[pl.ds(first,n,stride=2),:]=main
    table[pl.ds(first+1,n,stride=2),:]=tail
def widen(rows):
    up=rows.astype(f32)
    return up[:,:128],jnp.concatenate([up[:,128:],jnp.zeros((up.shape[0],104),f32)],axis=1)
def backward_kernel(places,src,dst,up_ref,pm_ref,pt_ref,mask_ref,rep_ref,t_ref,local_ref,out_ref,t_buf,sems,table,xs,ys,*accs):
    copies=fetch_operators(t_ref,t_buf,sems)
    xs[...]=jnp.zeros_like(xs)
    ys[...]=jnp.zeros_like(ys)
    for acc in accs:
        zero_fill(acc)
    m,t=widen(up_ref[...])
    store_rows(table,0,m,t)
    translate_runs(places,src,dst,True,copies,table,t_buf,xs,ys,accs)
    m,t=sum_rows(accs,0,64)
    local_ref[:,:128]=m
    local_ref[:,128:]=t[:,:24]
    def step(g,_):
        main,tail=sum_rows(accs,128+320*g,160)
        tail=(jnp.dot(tail.astype(bf16),rep_ref[...],preferred_element_type=f32)*mask_ref[...]).astype(bf16)
        packed=jnp.dot(pm_ref[...],main.astype(bf16),preferred_element_type=f32)+jnp.dot(pt_ref[...],tail,preferred_element_type=f32)
        out_ref[pl.ds(pl.multiple_of(192*g,192),192),:]=packed.astype(bf16)
        return 0
    lax.fori_loop(0,16,step,0,unroll=2)
def forward_kernel(places,src,dst,up_ref,came_ref,pm_ref,pt_ref,mask_ref,fold_ref,t_ref,own_ref,t_buf,sems,table,xs,ys,*accs):
    copies=fetch_operators(t_ref,t_buf,sems)
    xs[...]=jnp.zeros_like(xs)
    ys[...]=jnp.zeros_like(ys)
    for acc in accs:
        acc[...]=jnp.zeros_like(acc)
    m,t=widen(up_ref[...])
    store_rows(table,0,m,t)
    table[5248:5264,:]=jnp.zeros((16,128),f32)
    def unpack(g,_):
        rows=came_ref[pl.ds(pl.multiple_of(192*g,192),192),:]
        main=jnp.dot(pm_ref[...],rows,preferred_element_type=f32)
        tail=(jnp.dot(pt_ref[...],rows,preferred_element_type=f32)*mask_ref[...]).astype(bf16)
        tail=jnp.dot(tail,fold_ref[...],preferred_element_type=f32)
        store_rows(table,128+320*g,main,tail)
        return 0
    lax.fori_loop(0,16,unpack,0,unroll=4)
    translate_runs(places,src,dst,False,copies,table,t_buf,xs,ys,accs)
    m,t=sum_rows(accs,0,64)
    own_ref[:,:128]=m
    own_ref[:,128:]=t[:,:24]
SM=pl.BlockSpec(memory_space=pltpu.SMEM); VM=pl.BlockSpec(memory_space=pltpu.VMEM)
def scratch(rows,acc_rows):
    return [pltpu.VMEM((NOPS,152,152),bf16),pltpu.SemaphoreType.DMA((5,)),pltpu.VMEM((rows,128),f32),pltpu.VMEM((GROUP,32,128),f32),pltpu.VMEM((GROUP,32,128),f32)]+[pltpu.VMEM((acc_rows,128),f32)]*NACC
LIM=46*1024*1024
ANY=pl.BlockSpec(memory_space=pl.ANY)
def backward(places,src,dst,up,t):
    main,tail,mask,fold=pack_maps()
    c=lambda a,d: jnp.asarray(a.astype(np.float32),d)
    return pl.pallas_call(backward_kernel,in_specs=[SM]*3+[VM]*5+[ANY],out_specs=[VM,VM],
        out_shape=[jax.ShapeDtypeStruct((64,152),f32),jax.ShapeDtypeStruct((3072,128),bf16)],
        scratch_shapes=scratch(128,5312),compiler_params=pltpu.CompilerParams(vmem_limit_bytes=LIM),name="backward")(
        places,src,dst,up,c(main,bf16),c(tail,bf16),c(mask,f32),c(fold.T,bf16),t)
def forward(places,src,dst,up,came,t):
    main,tail,mask,fold=pack_maps()
    c=lambda a,d: jnp.asarray(a.astype(np.float32),d)
    return pl.pallas_call(forward_kernel,in_specs=[SM]*3+[VM]*6+[ANY],out_specs=VM,
        out_shape=jax.ShapeDtypeStruct((64,152),f32),
        scratch_shapes=scratch(5264,128),compiler_params=pltpu.CompilerParams(vmem_limit_bytes=LIM),name="forward")(
        places,src,dst,up,came,c(main.T,bf16),c(tail.T,bf16),c(mask,f32),c(fold,bf16),t)
def operator_kernel(m_ref,t_ref,s1,s2):
    part=pl.program_id(1)
    def turn(j,_):
        t=m_ref[j].T.astype(f32)
        s1[pl.ds(part*76+j,128,stride=153),:]=t[:,:128]
        s2[pl.ds(part*76+j,128,stride=153),0:24]=t[:,128:]
        return 0
    lax.fori_loop(0,76,turn,0,unroll=UN)
    @pl.when(part==1)
    def _():
        def collect(k,_):
            t_ref[k,:,0:128]=s1[pl.ds(k*153,152),:].astype(bf16)
            t_ref[k,:,128:152]=s2[pl.ds(k*153,152),:][:,:24].astype(bf16)
            return 0
        lax.fori_loop(0,128,collect,0,unroll=4)
UN=19
def operators(m):
    return pl.pallas_call(operator_kernel,grid=(3,2),in_specs=[pl.BlockSpec((76,152,128),lambda i,j:(j,0,i))],
      out_specs=pl.BlockSpec((128,152,152),lambda i,j:(i,0,0)),out_shape=jax.ShapeDtypeStruct((NOPS,152,152),bf16),
      scratch_shapes=[pltpu.VMEM((128*153,128),f32)]*2,
      compiler_params=pltpu.CompilerParams(vmem_limit_bytes=50*1024*1024),name="operators")(m)

def slot_rows(send):
    flat=jnp.pad(send,((0,0),(0,4)),constant_values=-1).reshape(1,3072)
    parts=[flat]
    split=send.reshape(128,4,5)
    for t in range(5):
        parts.append(jnp.pad(split[:,:,t],((0,0),(20,0)),constant_values=-1).reshape(1,3072))
    return jnp.concatenate(parts+[jnp.full((2,3072),-1,jnp.int32)])
def slot_hot(slot_ref):
    boxes=lax.broadcasted_iota(jnp.int32,(64,3072),0)
    return [jnp.where(boxes==slot_ref[b:b+1,:],1.0,0.0).astype(bf16) for b in range(6)]
def send_kernel(slot_ref,up_ref,rep_ref,out_ref):
    up=up_ref[...]
    tail=jnp.dot(jnp.concatenate([up[:,128:],jnp.zeros((64,104),bf16)],axis=1),rep_ref[...],preferred_element_type=f32)
    lane=lax.broadcasted_iota(jnp.int32,(64,128),1)
    values=[up[:,:128]]+[jnp.where((lane>=24*t)&(lane<24*t+24),tail,0.0).astype(bf16) for t in range(5)]
    hot=jnp.concatenate(slot_hot(slot_ref),axis=0)
    out_ref[...]=lax.dot_general(hot,jnp.concatenate(values,axis=0),(((0,),(0,)),((),())),preferred_element_type=f32).astype(bf16)
def pack_sends(slots,up):
    fold=pack_maps()[3]
    return pl.pallas_call(send_kernel,in_specs=[VM]*3,out_specs=VM,out_shape=jax.ShapeDtypeStruct((3072,128),bf16),
        compiler_params=pltpu.CompilerParams(vmem_limit_bytes=LIM),name="send")(slots,up,jnp.asarray(fold.T.astype(np.float32),bf16))
def finish_kernel(slot_ref,came_ref,local_ref,own_ref,c2e_ref,coarse_ref,parent_ref):
    hot=jnp.concatenate(slot_hot(slot_ref),axis=0)
    got=jnp.dot(hot,came_ref[...],preferred_element_type=f32)
    tail=got[64:128,0:24]
    for t in range(1,5):
        tail=tail+got[64+64*t:128+64*t,24*t:24*t+24]
    check=local_ref[...]+own_ref[...]+jnp.concatenate([got[:64],tail],axis=1)
    parent=jnp.dot(check,c2e_ref[...],precision=lax.Precision.HIGHEST,preferred_element_type=f32)+coarse_ref[...].astype(f32)
    parent_ref[...]=parent.astype(bf16)
def finish(slots,came,local,own,c2e,coarse):
    return pl.pallas_call(finish_kernel,in_specs=[VM]*6,out_specs=VM,out_shape=jax.ShapeDtypeStruct((64,152),bf16),
        compiler_params=pltpu.CompilerParams(vmem_limit_bytes=LIM),name="finish")(slots,came,local,own,c2e,coarse)
def pad_to(a,n,v):
    return jnp.concatenate([a,jnp.full((n-a.shape[0],),v,a.dtype)])
AXES=("slab","sub")
def shifted(x, by):
    count = lax.axis_size(AXES)
    return lax.ppermute(x, AXES, [(i, (i + by) % count) for i in range(count)])
def run_places(ids):
    run=jnp.arange(RUNS,dtype=jnp.int32)
    first=jnp.sum(jnp.where(pad_to(ids,RUNS,-1)[None,:]==run[:,None],OPCAP*run[None,:],0),axis=1)
    return jnp.where(run<NOPS,first,OPCAP*run)
def exchange(x):
    return lax.all_to_all(x.reshape(128,24,128),AXES,split_axis=0,concat_axis=0,tiled=True).reshape(3072,128)
def shards(leaves, coarse_local, m2m, m2l, c2e, l2l, send_box, pair_box, pair_partner, pair_op):
    width=152; box_count=64; edge=38
    front=jnp.concatenate([jnp.zeros((8*edge-LEAD,width),bf16),leaves[:LEAD]])
    front_sum=jnp.einsum("poj,oji->pi",front.reshape(edge,8,width),m2m,preferred_element_type=f32)
    arrived=shifted(front_sum,-1)
    ops=operators(jnp.transpose(m2l,(1,2,0)))
    own_rows=jnp.concatenate([leaves[LEAD:],jnp.zeros((LEAD,width),bf16)])
    up_sum=jnp.einsum("poj,oji->pi",own_rows.reshape(box_count,8,width),m2m,preferred_element_type=f32)
    up=up_sum.at[box_count-edge:].add(arrived).astype(bf16)
    slots=slot_rows(send_box.reshape(128,CAP))
    places=run_places(pair_op.reshape(NOPS,OPCAP)[:,0])
    partner=pad_to(2*jnp.where(pair_partner>=0,pair_partner,2624),SLOTS,2*2624)
    box=pad_to(2*pair_box,SLOTS,0)
    came=exchange(pack_sends(slots,up))
    local,to_owners=backward(places,box,partner,up,ops)
    returned=exchange(to_owners)
    own=forward(places,partner,box,up,came,ops)
    parent=finish(slots,returned,local,own,c2e,coarse_local)
    earlier=shifted(parent[box_count-edge:],1)
    head=jnp.einsum("pj,oji->poi",earlier,l2l,preferred_element_type=f32).reshape(8*edge,width)
    own_part=jnp.einsum("pj,oji->poi",parent,l2l,preferred_element_type=f32).reshape(8*box_count,width)
    leaf_local=jnp.concatenate([head[8*edge-LEAD:],own_part[:8*box_count-LEAD]])
    return (parent,leaf_local)


def solution(mesh):
    split = P(("slab", "sub"), None)
    flat = P(("slab", "sub"))
    return jax.shard_map(
        shards,
        mesh=mesh,
        in_specs=(split, split, P(), P(), P(), P(), split, flat, flat, flat),
        out_specs=(split, split),
        check_vma=False,
    )
```

time: 146 us -> 109 us (0.75)
  local copies, waits for them, and re-layouts: 42.9 us -> 9.96 us
  Pallas kernels: 65.2 us -> 60.3 us
  waiting for transfers between devices: 6.33 us -> 8.13 us
    unnamed x42 -> x30, local copies, waits for them, and re-layouts: 34.8 us -> 2.52 us
    pallas_call x3, Pallas kernels: 61.6 us -> 56.7 us  [the longest x1 23.5 us: operators(): pl.pallas_call(operator_kernel, grid=(3, 2), in_specs=[pl.BlockSpec((76,...]
    all_to_all x2, waiting for transfers between devices: 0.01 us -> 1.47 us  [exchange(): lax.all_to_all(x.reshape(128, 24, 128), AXES, split_axis=0, concat_axis=0...]
  transfers between devices with their start and end apart: 4 -> 4, of which waited for: 1 -> 2; matrix products, arithmetic and copies ran while one was open for 7% -> 9% of each run, Pallas kernels for 43% -> 52%
where the time goes in v2:
time: 109 us; the launch traced here: 108 us
  Pallas kernels  60.3 us (55%)
  starting transfers between devices  23.3 us (21%)
  local copies, waits for them, and re-layouts  9.96 us (9%)
  waiting for transfers between devices  8.13 us (7%)
  matrix products  3.9 us (4%)
  other arithmetic  1.7 us (2%)
    pallas_call x1, Pallas kernels, operators(): pl.pallas_call(operator_kernel, grid=(3, 2), in_specs=[pl.BlockSpec((76,...  23.5 us
    pallas_call x1, Pallas kernels, backward(): pl.pallas_call(backward_kernel, in_specs=[SM] * 3 + [VM] * 5 + [ANY], out...  18.9 us
    all_to_all x2, starting transfers between devices, exchange(): lax.all_to_all(x.reshape(128, 24, 128), AXES, split_axis=0, concat_axis=0...  14.4 us
    pallas_call x1, Pallas kernels, forward(): pl.pallas_call(forward_kernel, in_specs=[SM] * 3 + [VM] * 6 + [ANY], out_...  14.3 us
    ppermute x2, starting transfers between devices, shifted(): return lax.ppermute(x, AXES, [(i, (i + by) % count) for i in range(count)])  8.91 us
    ppermute x2, waiting for transfers between devices, shifted(): return lax.ppermute(x, AXES, [(i, (i + by) % count) for i in range(count)])  6.66 us
    unnamed x30, local copies, waits for them, and re-layouts  2.52 us
  transfers between devices with their start and end apart: 4, of which 2 were waited for; matrix products, arithmetic and copies ran while one was open for 9% of the time, Pallas kernels for 52%

profile of v2, /device:TPU:0, one launch (start us, length us, event | category | flops | bytes accessed | tf_op | source)
XLA Modules:
  0.0 108.4 jit_solution(5299845981842579529)
XLA Ops:
  0.6 1.0 slice.60
  1.6 0.1 copy.68
  1.8 1.3 %convolution_bitcast_fusion.1 = f32[38,152]{1,0:T(8,128)S(1)} fusion(bf16[8,152,152]{2,1,0:T(8,128)(2,1)} %param.23, bf16[38,8,152]{2,1,0:T(8,128)(2,1)S(1)} %pad_bitcast_fusion.1), kind=kOutput, calls=%fused_computation.1 | convolution fusion | flops 14047232 | bytes 485184 | tf_op jit(solution)/shard_map/poj,oji->pi/dot_general | solution.py:203
  3.1 8.3 %collective-permute-start = (f32[38,152]{1,0:T(8,128)S(1)}, f32[38,152]{1,0:T(8,128)S(1)}, u32[]{:S(2)}, u32[]{:S(2)}) collective-permute-start(f32[38,152]{1,0:T(8,128)S(1)} %convolution_bitcast_fusion.1), channel_id=1, source_target_pairs={{0,127},{1,0},{2,1},{3,2},{4,3},{5,4},{6,5},{7,6},{8,7},{9,8},{10,... | collective-permute-start | bytes 69320 | tf_op jit(solution)/shard_map/ppermute | solution.py:193
  11.4 1.0 slice.58
  12.4 0.7 broadcast_multiply_fusion
  13.3 0.7 reduce.2
  14.0 0.3 reshape_reshape.3
  14.3 0.6 fusion.8
  15.0 1.3 %convolution_bitcast_fusion = f32[64,152]{1,0:T(8,128)S(1)} fusion(bf16[8,152,152]{2,1,0:T(8,128)(2,1)} %param.23, bf16[64,8,152]{2,1,0:T(8,128)(2,1)S(1)} %pad_bitcast_fusion), kind=kOutput, calls=%fused_computation | convolution fusion | flops 23658496 | bytes 564224 | tf_op jit(solution)/shard_map/poj,oji->pi/dot_general | solution.py:207
  16.4 0.1 reshape.84
  16.5 0.1 reshape.85
  16.6 0.9 reshape.91
  17.6 0.1 copy.56
  17.8 0.1 copy.54
  17.9 0.1 copy.52
  18.0 0.1 copy.50
  18.1 0.1 copy.69
  18.4 0.1 reshape.86
  18.5 0.1 copy.70
  18.7 0.1 reshape.87
  18.8 0.1 copy.71
  19.0 0.1 reshape.88
  19.1 0.1 copy.72
  19.3 0.1 reshape.89
  19.4 0.1 copy.73
  19.6 0.1 reshape.90
  19.8 0.1 concatenate.23.slot_ref
  19.9 0.3 scatter-add.4
  20.2 0.7 copy-done.3
  21.0 1.9 %send.1 = bf16[3072,128]{1,0:T(8,128)(2,1)} custom-call(s32[8,3072]{1,0:T(8,128)S(1)} %concatenate.23.slot_ref, bf16[64,152]{1,0:T(8,128)(2,1)S(1)} %convert_element_type.3.up_ref, bf16[128,128]{1,0:T(8,128)(2,1)S(1)} %copy-done.3), custom_call_target="tpu_custom_call" | custom-call | tf_op jit(solution)/shard_map/send/pallas_call | solution.py:174
  22.9 4.6 %all-to-all-start.1 = ((bf16[128,24,128]{2,1,0:T(8,128)(2,1)}), bf16[128,24,128]{2,1,0:T(8,128)(2,1)S(1)}, u32[]{:S(2)}, u32[]{:S(2)}) async-start(bf16[128,24,128]{2,1,0:T(8,128)(2,1)} %bitcast.12), calls=%async_computation.1 | async-start | bytes 1572864 | tf_op jit(solution)/shard_map/all_to_all | solution.py:199
  27.5 0.1 slice_reduce_fusion
  27.7 23.5 %operators.1.t_ref = bf16[316,152,152]{2,1,0:T(8,128)(2,1)} custom-call(bf16[152,152,316]{2,1,0:T(8,128)(2,1)} %bitcast.36), custom_call_target="tpu_custom_call" | custom-call | tf_op jit(solution)/shard_map/operators/pallas_call | solution.py:150
  51.2 0.2 select_reduce_fusion
  51.5 18.9 %backward.1 = (f32[64,152]{1,0:T(8,128)S(1)}, bf16[3072,128]{1,0:T(8,128)(2,1)}) custom-call(s32[320]{0:T(512)S(1)} %fusion.7.places, s32[4160]{0:T(1024)S(1)} %concatenate.25.src.dst, s32[4160]{0:T(1024)S(1)} %concatenate.26.dst.src, bf16[64,152]{1,0:T(8,128)(2,1)S(1)} %convert_element_type.3.up_ref, bf16[192,160]{1,0:T(8,128)(2,1)S(1)} %copy-done.5, ...), custom_call_target="tpu_custom_call" | custom-call | tf_op jit(solution)/shard_map/backward/pallas_call | solution.py:122
  70.4 9.8 %all-to-all-start = ((bf16[128,24,128]{2,1,0:T(8,128)(2,1)}), bf16[128,24,128]{2,1,0:T(8,128)(2,1)S(1)}, u32[]{:S(2)}, u32[]{:S(2)}) async-start(bf16[128,24,128]{2,1,0:T(8,128)(2,1)} %bitcast.10), calls=%async_computation | async-start | bytes 1572864 | tf_op jit(solution)/shard_map/all_to_all | solution.py:199
  80.2 14.3 %forward.1.own_ref = f32[64,152]{1,0:T(8,128)S(1)} custom-call(s32[320]{0:T(512)S(1)} %fusion.7.places, s32[4160]{0:T(1024)S(1)} %concatenate.26.dst.src, s32[4160]{0:T(1024)S(1)} %concatenate.25.src.dst, bf16[64,152]{1,0:T(8,128)(2,1)S(1)} %convert_element_type.3.up_ref, bf16[3072,128]{1,0:T(8,128)(2,1)S(1)} %bitcast.34, bf16[160,192]{1,0:T(8,128)(2,1)S(1)} %copy-done.7, ...), custom_call_target="tpu_custom_call" | custom-call | tf_op jit(solution)/shard_map/forward/pallas_call | solution.py:129
  94.5 1.5 %all-to-all-done = bf16[128,24,128]{2,1,0:T(8,128)(2,1)S(1)} async-done(((bf16[128,24,128]{2,1,0:T(8,128)(2,1)}), bf16[128,24,128]{2,1,0:T(8,128)(2,1)S(1)}, u32[]{:S(2)}, u32[]{:S(2)}) %all-to-all-start) | async-done | bytes 786464 | tf_op jit(solution)/shard_map/all_to_all | solution.py:199
  96.0 1.8 %finish.1 = bf16[64,152]{1,0:T(8,128)(2,1)} custom-call(s32[8,3072]{1,0:T(8,128)S(1)} %concatenate.23.slot_ref, bf16[3072,128]{1,0:T(8,128)(2,1)S(1)} %bitcast.35, f32[64,152]{1,0:T(8,128)S(1)} %get-tuple-element.17.local_ref, f32[64,152]{1,0:T(8,128)S(1)} %forward.1.own_ref, f32[152,152]{1,0:T(8,128)S(1)} %copy-done.2, bf16[64,152]{1,0:T(8,128)(2,1)S(1)} %copy-done.9), custom_call_target="tpu_custom_call" | custom-call | tf_op jit(solution)/shard_map/finish/pallas_call | solution.py:186
  97.7 0.7 slice.71
  98.5 0.6 collective-permute-start.1
  99.1 1.0 fusion.2
  100.1 0.3 copy.80
  100.4 6.7 %collective-permute-done.1 = bf16[38,152]{1,0:T(8,128)(2,1)S(1)} collective-permute-done((bf16[38,152]{1,0:T(8,128)(2,1)S(1)}, bf16[38,152]{1,0:T(8,128)(2,1)S(1)}, u32[]{:S(2)}, u32[]{:S(2)}) %collective-permute-start.1) | collective-permute-done | bytes 11584 | tf_op jit(solution)/shard_map/ppermute | solution.py:193
  107.1 0.2 fusion.5
  107.3 0.1 copy.81
  107.5 0.9 copy.66
  (45 shorter events, 0.9 us)
Async XLA Ops:
  0.6 98.5 %copy-start = (bf16[8,152,152]{2,1,0:T(8,128)(2,1)S(1)}, bf16[8,152,152]{2,1,0:T(8,128)(2,1)}, u32[]{:S(2)}) copy-start(bf16[8,152,152]{2,1,0:T(8,128)(2,1)} %param.26) | copy-start | bytes 1108996
  3.1 16.8 %collective-permute-start = (f32[38,152]{1,0:T(8,128)S(1)}, f32[38,152]{1,0:T(8,128)S(1)}, u32[]{:S(2)}, u32[]{:S(2)}) collective-permute-start(f32[38,152]{1,0:T(8,128)S(1)} %convolution_bitcast_fusion.1), channel_id=1, source_target_pairs={{0,127},{1,0},{2,1},{3,2},{4,3},{5,4},{6,5},{7,6},{8,7},{9,8},{10,... | collective-permute-start | bytes 69320 | tf_op jit(solution)/shard_map/ppermute | solution.py:193
  16.3 34.9 %copy-start.10 = (s32[4108]{0:T(1024)S(1)}, s32[4108]{0:T(1024)}, u32[]{:S(2)}) copy-start(s32[4108]{0:T(1024)} %param.29) | copy-start | bytes 49300
  16.3 35.1 %copy-start.1 = (f32[160,128]{1,0:T(8,128)S(1)}, f32[160,128]{1,0:T(8,128)}, u32[]{:S(2)}) copy-start(f32[160,128]{1,0:T(8,128)} %constant.67.clone.mask_ref) | copy-start | bytes 245764
  16.3 35.1 %copy-start.4 = (bf16[192,160]{1,0:T(8,128)(2,1)S(1)}, bf16[192,160]{1,0:T(8,128)(2,1)}, u32[]{:S(2)}) copy-start(bf16[192,160]{1,0:T(8,128)(2,1)} %constant.66.clone.pt_ref) | copy-start | bytes 184324
  16.3 35.1 %copy-start.5 = (bf16[192,160]{1,0:T(8,128)(2,1)S(1)}, bf16[192,160]{1,0:T(8,128)(2,1)}, u32[]{:S(2)}) copy-start(bf16[192,160]{1,0:T(8,128)(2,1)} %constant.65.clone.pm_ref) | copy-start | bytes 184324
  20.2 0.8 copy-start.3
  22.9 47.5 %all-to-all-start.1 = ((bf16[128,24,128]{2,1,0:T(8,128)(2,1)}), bf16[128,24,128]{2,1,0:T(8,128)(2,1)S(1)}, u32[]{:S(2)}, u32[]{:S(2)}) async-start(bf16[128,24,128]{2,1,0:T(8,128)(2,1)} %bitcast.12), calls=%async_computation.1 | async-start | bytes 1572864 | tf_op jit(solution)/shard_map/all_to_all | solution.py:199
  27.7 52.5 %copy-start.6 = (bf16[160,192]{1,0:T(8,128)(2,1)S(1)}, bf16[160,192]{1,0:T(8,128)(2,1)}, u32[]{:S(2)}) copy-start(bf16[160,192]{1,0:T(8,128)(2,1)} %constant.69.clone.pt_ref) | copy-start | bytes 184324
  27.7 52.5 %copy-start.7 = (bf16[160,192]{1,0:T(8,128)(2,1)S(1)}, bf16[160,192]{1,0:T(8,128)(2,1)}, u32[]{:S(2)}) copy-start(bf16[160,192]{1,0:T(8,128)(2,1)} %constant.68.clone.pm_ref) | copy-start | bytes 184324
  27.7 52.5 %copy-start.8 = (bf16[128,128]{1,0:T(8,128)(2,1)S(1)}, bf16[128,128]{1,0:T(8,128)(2,1)}, u32[]{:S(2)}) copy-start(bf16[128,128]{1,0:T(8,128)(2,1)} %constant.70.clone.fold_ref) | copy-start | bytes 98308
  51.4 44.5 %copy-start.2 = (f32[152,152]{1,0:T(8,128)S(1)}, f32[152,152]{1,0:T(8,128)}, u32[]{:S(2)}) copy-start(f32[152,152]{1,0:T(8,128)} %c2e_ref.1) | copy-start | bytes 277252
  51.4 44.5 %copy-start.9 = (bf16[64,152]{1,0:T(8,128)(2,1)S(1)}, bf16[64,152]{1,0:T(8,128)(2,1)}, u32[]{:S(2)}) copy-start(bf16[64,152]{1,0:T(8,128)(2,1)} %coarse_ref.1) | copy-start | bytes 58372
  70.4 25.6 %all-to-all-start = ((bf16[128,24,128]{2,1,0:T(8,128)(2,1)}), bf16[128,24,128]{2,1,0:T(8,128)(2,1)S(1)}, u32[]{:S(2)}, u32[]{:S(2)}) async-start(bf16[128,24,128]{2,1,0:T(8,128)(2,1)} %bitcast.10), calls=%async_computation | async-start | bytes 1572864 | tf_op jit(solution)/shard_map/all_to_all | solution.py:199
  98.5 8.6 %collective-permute-start.1 = (bf16[38,152]{1,0:T(8,128)(2,1)S(1)}, bf16[38,152]{1,0:T(8,128)(2,1)S(1)}, u32[]{:S(2)}, u32[]{:S(2)}) collective-permute-start(bf16[38,152]{1,0:T(8,128)(2,1)S(1)} %slice.71), channel_id=1, source_target_pairs={{0,1},{1,2},{2,3},{3,4},{4,5},{5,6},{6,7},{7,8},{8,9},{9,10},{10,1... | collective-permute-start | bytes 34664 | tf_op jit(solution)/shard_map/ppermute | solution.py:193

commit v3 on v2

--- a/solution.py
+++ b/solution.py
@@ -131,60 +131,100 @@
         scratch_shapes=scratch(5264,128),compiler_params=pltpu.CompilerParams(vmem_limit_bytes=LIM),name="forward")(
         places,src,dst,up,came,c(main.T,bf16),c(tail.T,bf16),c(mask,f32),c(fold,bf16),t)
 def operator_kernel(m_ref,t_ref,s1,s2):
-    part=pl.program_id(1)
-    def turn(j,_):
-        t=m_ref[j].T.astype(f32)
-        s1[pl.ds(part*76+j,128,stride=153),:]=t[:,:128]
-        s2[pl.ds(part*76+j,128,stride=153),0:24]=t[:,128:]
-        return 0
-    lax.fori_loop(0,76,turn,0,unroll=UN)
-    @pl.when(part==1)
-    def _():
-        def collect(k,_):
-            t_ref[k,:,0:128]=s1[pl.ds(k*153,152),:].astype(bf16)
-            t_ref[k,:,128:152]=s2[pl.ds(k*153,152),:][:,:24].astype(bf16)
+    block=pl.program_id(0); part=pl.program_id(1)
+    def turn(n):
+        eye=(lax.broadcasted_iota(jnp.int32,(n,n),0)==lax.broadcasted_iota(jnp.int32,(n,n),1)).astype(bf16)
+        def body(g,_):
+            for u in range(19):
+                j=19*g+u
+                if u%3==2:
+                    t=lax.dot_general(eye,m_ref[j,:,0:n],(((1,),(1,)),((),())),preferred_element_type=f32)
+                else:
+                    t=m_ref[j,:,0:n].T.astype(f32)
+                s1[pl.ds(part*76+j,n,stride=153),:]=t[:,:128]
+                s2[pl.ds(part*76+j,n,stride=153),0:24]=t[:,128:]
             return 0
-        lax.fori_loop(0,128,collect,0,unroll=4)
-UN=19
+        lax.fori_loop(0,4,body,0)
+    def collect(n):
+        def body(q,_):
+            for u in range(4):
+                k=4*q+u
+                t_ref[k,:,0:128]=s1[pl.ds(k*153,152),:].astype(bf16)
+                t_ref[k,:,128:152]=s2[pl.ds(k*153,152),:][:,:24].astype(bf16)
+            return 0
+        lax.fori_loop(0,n//4,body,0)
+    @pl.when(block<2)
+    def _():
+        turn(128)
+    @pl.when(block==2)
+    def _():
+        turn(64)
+    @pl.when((part==1)&(block<2))
+    def _():
+        collect(128)
+    @pl.when((part==1)&(block==2))
+    def _():
+        collect(60)
 def operators(m):
     return pl.pallas_call(operator_kernel,grid=(3,2),in_specs=[pl.BlockSpec((76,152,128),lambda i,j:(j,0,i))],
       out_specs=pl.BlockSpec((128,152,152),lambda i,j:(i,0,0)),out_shape=jax.ShapeDtypeStruct((NOPS,152,152),bf16),
       scratch_shapes=[pltpu.VMEM((128*153,128),f32)]*2,
       compiler_params=pltpu.CompilerParams(vmem_limit_bytes=50*1024*1024),name="operators")(m)
 
-def slot_rows(send):
-    flat=jnp.pad(send,((0,0),(0,4)),constant_values=-1).reshape(1,3072)
-    parts=[flat]
-    split=send.reshape(128,4,5)
+EDGE=38
+def gather_kernel(leaf_ref,m2m_ref,front_ref,own_ref):
+    rows=leaf_ref[...].astype(f32).T.astype(bf16)
+    box=lax.broadcasted_iota(jnp.int32,(72,512),0)
+    row=lax.broadcasted_iota(jnp.int32,(72,512),1)
+    total=jnp.zeros((72,152),f32)
+    for c in range(8):
+        hot=jnp.where(row==8*box+(c-4),1.0,0.0).astype(bf16)
+        child=jnp.dot(hot,rows,preferred_element_type=f32).astype(bf16)
+        total=total+jnp.dot(child,m2m_ref[c],preferred_element_type=f32)
+    front_ref[...]=total[:EDGE]
+    own_ref[...]=jnp.concatenate([total[EDGE:65],jnp.zeros((37,152),f32)],axis=0)
+def gather_children(leaf_t,m2m):
+    return pl.pallas_call(gather_kernel,in_specs=[VM]*2,out_specs=[VM]*2,
+        out_shape=[jax.ShapeDtypeStruct((EDGE,152),f32),jax.ShapeDtypeStruct((64,152),f32)],
+        compiler_params=pltpu.CompilerParams(vmem_limit_bytes=16*1024*1024),name="gather")(leaf_t,m2m)
+def slot_hot(index_ref,g):
+    boxes=lax.broadcasted_iota(jnp.int32,(64,192),0).astype(f32)+1.0
+    return jnp.concatenate([jnp.where(boxes==index_ref[16*b+g:16*b+g+1,:],1.0,0.0).astype(bf16) for b in range(6)],axis=0)
+def send_kernel(send_ref,own_ref,arrived_ref,pm_ref,pt_ref,rep_ref,out_ref,up_ref,index_ref):
+    plus=(send_ref[...]+1).astype(f32)
+    plus=jnp.concatenate([plus[:,160*g:160*g+160] for g in range(16)],axis=0)
+    slot=lax.rem(lax.broadcasted_iota(jnp.int32,(16,160),1),5)
+    index_ref[0:16,:]=jnp.dot(plus.astype(bf16),pm_ref[...],preferred_element_type=f32)
     for t in range(5):
-        parts.append(jnp.pad(split[:,:,t],((0,0),(20,0)),constant_values=-1).reshape(1,3072))
-    return jnp.concatenate(parts+[jnp.full((2,3072),-1,jnp.int32)])
-def slot_hot(slot_ref):
-    boxes=lax.broadcasted_iota(jnp.int32,(64,3072),0)
-    return [jnp.where(boxes==slot_ref[b:b+1,:],1.0,0.0).astype(bf16) for b in range(6)]
-def send_kernel(slot_ref,up_ref,rep_ref,out_ref):
-    up=up_ref[...]
+        index_ref[16*t+16:16*t+32,:]=jnp.dot(jnp.where(slot==t,plus,0.0).astype(bf16),pt_ref[...],preferred_element_type=f32)
+    up=(own_ref[...]+jnp.concatenate([jnp.zeros((64-EDGE,152),f32),arrived_ref[...]],axis=0)).astype(bf16)
+    up_ref[...]=up
     tail=jnp.dot(jnp.concatenate([up[:,128:],jnp.zeros((64,104),bf16)],axis=1),rep_ref[...],preferred_element_type=f32)
     lane=lax.broadcasted_iota(jnp.int32,(64,128),1)
-    values=[up[:,:128]]+[jnp.where((lane>=24*t)&(lane<24*t+24),tail,0.0).astype(bf16) for t in range(5)]
-    hot=jnp.concatenate(slot_hot(slot_ref),axis=0)
-    out_ref[...]=lax.dot_general(hot,jnp.concatenate(values,axis=0),(((0,),(0,)),((),())),preferred_element_type=f32).astype(bf16)
-def pack_sends(slots,up):
-    fold=pack_maps()[3]
-    return pl.pallas_call(send_kernel,in_specs=[VM]*3,out_specs=VM,out_shape=jax.ShapeDtypeStruct((3072,128),bf16),
-        compiler_params=pltpu.CompilerParams(vmem_limit_bytes=LIM),name="send")(slots,up,jnp.asarray(fold.T.astype(np.float32),bf16))
-def finish_kernel(slot_ref,came_ref,local_ref,own_ref,c2e_ref,coarse_ref,parent_ref):
-    hot=jnp.concatenate(slot_hot(slot_ref),axis=0)
-    got=jnp.dot(hot,came_ref[...],preferred_element_type=f32)
+    values=jnp.concatenate([up[:,:128]]+[jnp.where((lane>=24*t)&(lane<24*t+24),tail,0.0).astype(bf16) for t in range(5)],axis=0)
+    for g in range(16):
+        out_ref[192*g:192*g+192,:]=lax.dot_general(slot_hot(index_ref,g),values,(((0,),(0,)),((),())),preferred_element_type=f32).astype(bf16)
+def pack_sends(send,own,arrived):
+    main,tail,mask,fold=pack_maps()
+    c=lambda a: jnp.asarray(a.astype(np.float32),bf16)
+    return pl.pallas_call(send_kernel,in_specs=[VM]*6,out_specs=[VM]*3,
+        out_shape=[jax.ShapeDtypeStruct((3072,128),bf16),jax.ShapeDtypeStruct((64,152),bf16),jax.ShapeDtypeStruct((96,192),f32)],
+        compiler_params=pltpu.CompilerParams(vmem_limit_bytes=16*1024*1024),name="send")(send,own,arrived,c(main.T),c(tail.T),c(fold.T))
+def finish_kernel(index_ref,came_ref,local_ref,own_ref,c2e_ref,coarse_ref,parent_ref,edge_ref):
+    got=jnp.zeros((384,128),f32)
+    for g in range(16):
+        got=got+jnp.dot(slot_hot(index_ref,g),came_ref[192*g:192*g+192,:],preferred_element_type=f32)
     tail=got[64:128,0:24]
     for t in range(1,5):
         tail=tail+got[64+64*t:128+64*t,24*t:24*t+24]
     check=local_ref[...]+own_ref[...]+jnp.concatenate([got[:64],tail],axis=1)
-    parent=jnp.dot(check,c2e_ref[...],precision=lax.Precision.HIGHEST,preferred_element_type=f32)+coarse_ref[...].astype(f32)
-    parent_ref[...]=parent.astype(bf16)
-def finish(slots,came,local,own,c2e,coarse):
-    return pl.pallas_call(finish_kernel,in_specs=[VM]*6,out_specs=VM,out_shape=jax.ShapeDtypeStruct((64,152),bf16),
-        compiler_params=pltpu.CompilerParams(vmem_limit_bytes=LIM),name="finish")(slots,came,local,own,c2e,coarse)
+    parent=(jnp.dot(check,c2e_ref[...],precision=lax.Precision.HIGHEST,preferred_element_type=f32)+coarse_ref[...].astype(f32)).astype(bf16)
+    parent_ref[...]=parent
+    edge_ref[...]=parent[64-EDGE:]
+def finish(index,came,local,own,c2e,coarse):
+    return pl.pallas_call(finish_kernel,in_specs=[VM]*6,out_specs=[VM]*2,
+        out_shape=[jax.ShapeDtypeStruct((64,152),bf16),jax.ShapeDtypeStruct((EDGE,152),bf16)],
+        compiler_params=pltpu.CompilerParams(vmem_limit_bytes=16*1024*1024),name="finish")(index,came,local,own,c2e,coarse)
 def pad_to(a,n,v):
     return jnp.concatenate([a,jnp.full((n-a.shape[0],),v,a.dtype)])
 AXES=("slab","sub")
@@ -198,24 +238,21 @@
 def exchange(x):
     return lax.all_to_all(x.reshape(128,24,128),AXES,split_axis=0,concat_axis=0,tiled=True).reshape(3072,128)
 def shards(leaves, coarse_local, m2m, m2l, c2e, l2l, send_box, pair_box, pair_partner, pair_op):
-    width=152; box_count=64; edge=38
-    front=jnp.concatenate([jnp.zeros((8*edge-LEAD,width),bf16),leaves[:LEAD]])
-    front_sum=jnp.einsum("poj,oji->pi",front.reshape(edge,8,width),m2m,preferred_element_type=f32)
+    width=152; box_count=64; edge=EDGE
+    ops=operators(jnp.transpose(m2l,(1,2,0)))
+    front_sum,own_sum=gather_children(leaves.T,m2m)
     arrived=shifted(front_sum,-1)
-    ops=operators(jnp.transpose(m2l,(1,2,0)))
-    own_rows=jnp.concatenate([leaves[LEAD:],jnp.zeros((LEAD,width),bf16)])
-    up_sum=jnp.einsum("poj,oji->pi",own_rows.reshape(box_count,8,width),m2m,preferred_element_type=f32)
-    up=up_sum.at[box_count-edge:].add(arrived).astype(bf16)
-    slots=slot_rows(send_box.reshape(128,CAP))
     places=run_places(pair_op.reshape(NOPS,OPCAP)[:,0])
     partner=pad_to(2*jnp.where(pair_partner>=0,pair_partner,2624),SLOTS,2*2624)
     box=pad_to(2*pair_box,SLOTS,0)
-    came=exchange(pack_sends(slots,up))
+    arrived,ops=lax.optimization_barrier((arrived,ops))
+    packed,up,index=pack_sends(send_box,own_sum,arrived)
+    came=exchange(packed)
     local,to_owners=backward(places,box,partner,up,ops)
     returned=exchange(to_owners)
     own=forward(places,partner,box,up,came,ops)
-    parent=finish(slots,returned,local,own,c2e,coarse_local)
-    earlier=shifted(parent[box_count-edge:],1)
+    parent,edges=finish(index,returned,local,own,c2e,coarse_local)
+    earlier=shifted(edges,1)
     head=jnp.einsum("pj,oji->poi",earlier,l2l,preferred_element_type=f32).reshape(8*edge,width)
     own_part=jnp.einsum("pj,oji->poi",parent,l2l,preferred_element_type=f32).reshape(8*box_count,width)
     leaf_local=jnp.concatenate([head[8*edge-LEAD:],own_part[:8*box_count-LEAD]])

time: 109 us -> 98.2 us (0.901)
  local copies, waits for them, and re-layouts: 9.96 us -> 3.82 us
  matrix products: 3.9 us -> 1.21 us
    slice x9 -> x0, local copies, waits for them, and re-layouts: 3.9 us -> none  [the longest x6 1.21 us: slot_rows(): split[:, :, t]]
    dot_general x2 -> x0, matrix products: 2.68 us -> none  [the longest x1 1.35 us: shards(): jnp.einsum('poj,oji->pi', own_rows.reshape(box_count, 8, width), m2m, pre...]
    pallas_call x1, Pallas kernels: 23.5 us -> 21.5 us  [operators(): pl.pallas_call(operator_kernel, grid=(3, 2), in_specs=[pl.BlockSpec((76,...]
    pallas_call x2 -> x3, Pallas kernels: 3.65 us -> 5.12 us  [the longest x1 2.22 us: pack_sends(): pl.pallas_call(send_kernel, in_specs=[VM] * 6, out_specs=[VM] * 3, out_sh...]
    unnamed x30 -> x31, local copies, waits for them, and re-layouts: 2.52 us -> 3.01 us
  transfers between devices with their start and end apart: 4 -> 4, of which waited for: 2 -> 2; matrix products, arithmetic and copies ran while one was open for 9% -> 3% of each run, Pallas kernels for 52% -> 55%
where the time goes in v3:
time: 98.2 us; the launch traced here: 98 us
  Pallas kernels  59.3 us (60%)
  starting transfers between devices  23.8 us (24%)
  waiting for transfers between devices  8.02 us (8%)
  local copies, waits for them, and re-layouts  3.82 us (4%)
  matrix products  1.21 us (1%)
    pallas_call x1, Pallas kernels, operators(): pl.pallas_call(operator_kernel, grid=(3, 2), in_specs=[pl.BlockSpec((76,...  21.5 us
    pallas_call x1, Pallas kernels, backward(): pl.pallas_call(backward_kernel, in_specs=[SM] * 3 + [VM] * 5 + [ANY], out...  18.3 us
    all_to_all x2, starting transfers between devices, exchange(): lax.all_to_all(x.reshape(128, 24, 128), AXES, split_axis=0, concat_axis=0...  14.9 us
    pallas_call x1, Pallas kernels, forward(): pl.pallas_call(forward_kernel, in_specs=[SM] * 3 + [VM] * 6 + [ANY], out_...  14.4 us
    ppermute x2, starting transfers between devices, shifted(): return lax.ppermute(x, AXES, [(i, (i + by) % count) for i in range(count)])  8.91 us
    ppermute x2, waiting for transfers between devices, shifted(): return lax.ppermute(x, AXES, [(i, (i + by) % count) for i in range(count)])  6.66 us
    unnamed x31, local copies, waits for them, and re-layouts  3.01 us
    pallas_call x1, Pallas kernels, pack_sends(): pl.pallas_call(send_kernel, in_specs=[VM] * 6, out_specs=[VM] * 3, out_sh...  2.22 us
  transfers between devices with their start and end apart: 4, of which 2 were waited for; matrix products, arithmetic and copies ran while one was open for 3% of the time, Pallas kernels for 55%

profile of v3, /device:TPU:0, one launch (start us, length us, event | category | flops | bytes accessed | tf_op | source)
XLA Modules:
  0.0 98.0 jit_solution(6240000061037919801)
XLA Ops:
  0.6 0.0 copy-start
  0.6 0.0 copy-start.1
  0.7 1.1 %copy-done.1 = bf16[8,152,152]{2,1,0:T(8,128)(2,1)S(1)} copy-done((bf16[8,152,152]{2,1,0:T(8,128)(2,1)S(1)}, bf16[8,152,152]{2,1,0:T(8,128)(2,1)}, u32[]{:S(2)}) %copy-start.1) | copy-done | bytes 369688
  1.8 0.0 copy-start.5
  1.8 0.9 copy-done.5
  2.7 0.0 copy-start.12
  2.7 0.0 copy-start.13
  2.7 0.0 copy-start.2
  2.7 0.0 copy-start.8
  2.8 0.0 copy-start.9
  2.8 1.0 gather.1
  3.7 8.3 %collective-permute-start = (f32[38,152]{1,0:T(8,128)S(1)}, f32[38,152]{1,0:T(8,128)S(1)}, u32[]{:S(2)}, u32[]{:S(2)}) collective-permute-start(f32[38,152]{1,0:T(8,128)S(1)} %get-tuple-element.14), channel_id=1, source_target_pairs={{0,127},{1,0},{2,1},{3,2},{4,3},{5,4},{6,5},{7,6},{8,7},{9,8},{10,... | collective-permute-start | bytes 69320 | tf_op jit(solution)/shard_map/ppermute | solution.py:233
  12.0 0.7 broadcast_multiply_fusion
  12.7 21.5 %operators.1.t_ref = bf16[316,152,152]{2,1,0:T(8,128)(2,1)} custom-call(bf16[152,152,316]{2,1,0:T(8,128)(2,1)} %bitcast.23), custom_call_target="tpu_custom_call" | custom-call | tf_op jit(solution)/shard_map/operators/pallas_call | solution.py:169
  34.2 0.0 copy-done.14
  34.2 0.2 reshape.31
  34.4 0.0 collective-permute-done.arrived_ref
  34.4 0.0 copy-done.3
  34.4 0.0 copy-done.4
  34.4 0.0 copy-done.7
  34.5 0.0 copy-done.12
  34.5 2.2 %send.1 = (bf16[3072,128]{1,0:T(8,128)(2,1)}, bf16[64,152]{1,0:T(8,128)(2,1)S(1)}, f32[96,192]{1,0:T(8,128)S(1)}) custom-call(s32[1,2560]{1,0:T(1,128)S(1)} %copy-done.12, f32[64,152]{1,0:T(8,128)S(1)} %get-tuple-element.13.own_ref, f32[38,152]{1,0:T(8,128)S(1)} %collective-permute-done.arrived_ref, bf16[160,192]{1,0:T(8,128)(2,1)S(1)} %copy-done.3, ...), custom_call_target="tpu_custom_call" | custom-call | tf_op jit(solution)/shard_map/send/pallas_call | solution.py:210
  36.7 4.6 %all-to-all-start.1 = ((bf16[128,24,128]{2,1,0:T(8,128)(2,1)}), bf16[128,24,128]{2,1,0:T(8,128)(2,1)S(1)}, u32[]{:S(2)}, u32[]{:S(2)}) async-start(bf16[128,24,128]{2,1,0:T(8,128)(2,1)} %bitcast.4), calls=%async_computation.1 | async-start | bytes 1572864 | tf_op jit(solution)/shard_map/all_to_all | solution.py:239
  41.3 0.1 slice_reduce_fusion
  41.5 0.0 copy-done.13
  41.5 0.2 select_reduce_fusion
  41.7 0.0 copy-done.2
  41.7 0.0 copy-done.8
  41.7 0.0 copy-done.9
  41.7 0.0 copy-start.6
  41.7 0.0 copy-start.11
  41.7 18.3 %backward.1 = (f32[64,152]{1,0:T(8,128)S(1)}, bf16[3072,128]{1,0:T(8,128)(2,1)}) custom-call(s32[320]{0:T(512)S(1)} %fusion.5.places, s32[4160]{0:T(1024)S(1)} %concatenate.13.src.dst, s32[4160]{0:T(1024)S(1)} %concatenate.14.dst.src, bf16[64,152]{1,0:T(8,128)(2,1)S(1)} %get-tuple-element.17.up_ref, bf16[192,160]{1,0:T(8,128)(2,1)S(1)} %copy-done.8, ...), custom_call_target="tpu_custom_call" | custom-call | tf_op jit(solution)/shard_map/backward/pallas_call | solution.py:122
  60.0 0.0 all-to-all-done.1
  60.1 10.3 %all-to-all-start = ((bf16[128,24,128]{2,1,0:T(8,128)(2,1)}), bf16[128,24,128]{2,1,0:T(8,128)(2,1)S(1)}, u32[]{:S(2)}, u32[]{:S(2)}) async-start(bf16[128,24,128]{2,1,0:T(8,128)(2,1)} %bitcast.2), calls=%async_computation | async-start | bytes 1572864 | tf_op jit(solution)/shard_map/all_to_all | solution.py:239
  70.3 0.0 copy-done.10
  70.3 14.4 %forward.1.own_ref = f32[64,152]{1,0:T(8,128)S(1)} custom-call(s32[320]{0:T(512)S(1)} %fusion.5.places, s32[4160]{0:T(1024)S(1)} %concatenate.14.dst.src, s32[4160]{0:T(1024)S(1)} %concatenate.13.src.dst, bf16[64,152]{1,0:T(8,128)(2,1)S(1)} %get-tuple-element.17.up_ref, bf16[3072,128]{1,0:T(8,128)(2,1)S(1)} %bitcast.20, bf16[160,192]{1,0:T(8,128)(2,1)S(1)} %copy-done.3, ...), custom_call_target="tpu_custom_call" | custom-call | tf_op jit(solution)/shard_map/forward/pallas_call | solution.py:129
  84.8 1.4 %all-to-all-done = bf16[128,24,128]{2,1,0:T(8,128)(2,1)S(1)} async-done(((bf16[128,24,128]{2,1,0:T(8,128)(2,1)}), bf16[128,24,128]{2,1,0:T(8,128)(2,1)S(1)}, u32[]{:S(2)}, u32[]{:S(2)}) %all-to-all-start) | async-done | bytes 786464 | tf_op jit(solution)/shard_map/all_to_all | solution.py:239
  86.1 0.0 copy-done.6
  86.1 0.0 copy-done.11
  86.1 1.9 %finish.1 = (bf16[64,152]{1,0:T(8,128)(2,1)}, bf16[38,152]{1,0:T(8,128)(2,1)S(1)}) custom-call(f32[96,192]{1,0:T(8,128)S(1)} %get-tuple-element.16.index_ref, bf16[3072,128]{1,0:T(8,128)(2,1)S(1)} %bitcast.21, f32[64,152]{1,0:T(8,128)S(1)} %get-tuple-element.20.local_ref, f32[64,152]{1,0:T(8,128)S(1)} %forward.1.own_ref, f32[152,152]{1,0:T(8,128)S(1)} %copy-done.6, ...), custom_call_target="tpu_custom_call" | custom-call | tf_op jit(solution)/shard_map/finish/pallas_call | solution.py:225
  88.1 0.6 collective-permute-start.1
  88.7 0.0 copy-done
  88.7 1.0 %fusion = f32[64,8,152]{2,0,1:T(8,128)S(1)} fusion(bf16[8,152,152]{2,1,0:T(8,128)(2,1)S(1)} %copy-done, bf16[64,152]{1,0:T(8,128)(2,1)} %get-tuple-element.26), kind=kOutput, calls=%fused_computation.7 | convolution fusion | flops 23658496 | bytes 700416 | tf_op jit(solution)/shard_map/pj,oji->poi/dot_general | solution.py:257
  89.7 0.3 copy.31
  90.1 6.7 %collective-permute-done.1 = bf16[38,152]{1,0:T(8,128)(2,1)S(1)} collective-permute-done((bf16[38,152]{1,0:T(8,128)(2,1)S(1)}, bf16[38,152]{1,0:T(8,128)(2,1)S(1)}, u32[]{:S(2)}, u32[]{:S(2)}) %collective-permute-start.1) | collective-permute-done | bytes 11584 | tf_op jit(solution)/shard_map/ppermute | solution.py:233
  96.7 0.2 fusion.3
  96.9 0.1 copy.32
  97.2 0.9 copy.28
  (14 shorter events, 0.1 us)
Async XLA Ops:
  0.6 88.1 %copy-start = (bf16[8,152,152]{2,1,0:T(8,128)(2,1)S(1)}, bf16[8,152,152]{2,1,0:T(8,128)(2,1)}, u32[]{:S(2)}) copy-start(bf16[8,152,152]{2,1,0:T(8,128)(2,1)} %param.26) | copy-start | bytes 1108996
  0.6 1.1 %copy-start.1 = (bf16[8,152,152]{2,1,0:T(8,128)(2,1)S(1)}, bf16[8,152,152]{2,1,0:T(8,128)(2,1)}, u32[]{:S(2)}) copy-start(bf16[8,152,152]{2,1,0:T(8,128)(2,1)} %m2m_ref.1) | copy-start | bytes 1108996
  1.8 0.9 copy-start.5
  2.7 31.5 %copy-start.14 = (s32[4108]{0:T(1024)S(1)}, s32[4108]{0:T(1024)}, u32[]{:S(2)}) copy-start(s32[4108]{0:T(1024)} %param.30) | copy-start | bytes 49300
  2.7 31.7 %copy-start.3 = (bf16[160,192]{1,0:T(8,128)(2,1)S(1)}, bf16[160,192]{1,0:T(8,128)(2,1)}, u32[]{:S(2)}) copy-start(bf16[160,192]{1,0:T(8,128)(2,1)} %constant.11.clone.pm_ref) | copy-start | bytes 184324
  2.7 31.7 %copy-start.4 = (bf16[160,192]{1,0:T(8,128)(2,1)S(1)}, bf16[160,192]{1,0:T(8,128)(2,1)}, u32[]{:S(2)}) copy-start(bf16[160,192]{1,0:T(8,128)(2,1)} %constant.12.clone.pt_ref) | copy-start | bytes 184324
  2.7 31.7 %copy-start.7 = (bf16[128,128]{1,0:T(8,128)(2,1)S(1)}, bf16[128,128]{1,0:T(8,128)(2,1)}, u32[]{:S(2)}) copy-start(bf16[128,128]{1,0:T(8,128)(2,1)} %constant.13.clone.rep_ref) | copy-start | bytes 98308
  2.7 31.7 %copy-start.12 = (s32[1,2560]{1,0:T(1,128)S(1)}, s32[1,2560]{1,0:T(1,128)}, u32[]{:S(2)}) copy-start(s32[1,2560]{1,0:T(1,128)} %send_ref.1) | copy-start | bytes 30724
  2.7 38.8 %copy-start.13 = (s32[4108]{0:T(1024)S(1)}, s32[4108]{0:T(1024)}, u32[]{:S(2)}) copy-start(s32[4108]{0:T(1024)} %param.29) | copy-start | bytes 49300
  2.7 39.0 %copy-start.2 = (f32[160,128]{1,0:T(8,128)S(1)}, f32[160,128]{1,0:T(8,128)}, u32[]{:S(2)}) copy-start(f32[160,128]{1,0:T(8,128)} %constant.36.clone.mask_ref) | copy-start | bytes 245764
  2.7 39.0 %copy-start.8 = (bf16[192,160]{1,0:T(8,128)(2,1)S(1)}, bf16[192,160]{1,0:T(8,128)(2,1)}, u32[]{:S(2)}) copy-start(bf16[192,160]{1,0:T(8,128)(2,1)} %constant.34.clone.pm_ref) | copy-start | bytes 184324
  2.8 39.0 %copy-start.9 = (bf16[192,160]{1,0:T(8,128)(2,1)S(1)}, bf16[192,160]{1,0:T(8,128)(2,1)}, u32[]{:S(2)}) copy-start(bf16[192,160]{1,0:T(8,128)(2,1)} %constant.35.clone.pt_ref) | copy-start | bytes 184324
  3.7 30.7 %collective-permute-start = (f32[38,152]{1,0:T(8,128)S(1)}, f32[38,152]{1,0:T(8,128)S(1)}, u32[]{:S(2)}, u32[]{:S(2)}) collective-permute-start(f32[38,152]{1,0:T(8,128)S(1)} %get-tuple-element.14), channel_id=1, source_target_pairs={{0,127},{1,0},{2,1},{3,2},{4,3},{5,4},{6,5},{7,6},{8,7},{9,8},{10,... | collective-permute-start | bytes 69320 | tf_op jit(solution)/shard_map/ppermute | solution.py:233
  34.2 36.1 %copy-start.10 = (bf16[128,128]{1,0:T(8,128)(2,1)S(1)}, bf16[128,128]{1,0:T(8,128)(2,1)}, u32[]{:S(2)}) copy-start(bf16[128,128]{1,0:T(8,128)(2,1)} %constant.37.clone.fold_ref) | copy-start | bytes 98308
  36.7 23.4 %all-to-all-start.1 = ((bf16[128,24,128]{2,1,0:T(8,128)(2,1)}), bf16[128,24,128]{2,1,0:T(8,128)(2,1)S(1)}, u32[]{:S(2)}, u32[]{:S(2)}) async-start(bf16[128,24,128]{2,1,0:T(8,128)(2,1)} %bitcast.4), calls=%async_computation.1 | async-start | bytes 1572864 | tf_op jit(solution)/shard_map/all_to_all | solution.py:239
  41.7 44.4 %copy-start.6 = (f32[152,152]{1,0:T(8,128)S(1)}, f32[152,152]{1,0:T(8,128)}, u32[]{:S(2)}) copy-start(f32[152,152]{1,0:T(8,128)} %c2e_ref.1) | copy-start | bytes 277252
  41.7 44.4 %copy-start.11 = (bf16[64,152]{1,0:T(8,128)(2,1)S(1)}, bf16[64,152]{1,0:T(8,128)(2,1)}, u32[]{:S(2)}) copy-start(bf16[64,152]{1,0:T(8,128)(2,1)} %coarse_ref.1) | copy-start | bytes 58372
  60.1 26.1 %all-to-all-start = ((bf16[128,24,128]{2,1,0:T(8,128)(2,1)}), bf16[128,24,128]{2,1,0:T(8,128)(2,1)S(1)}, u32[]{:S(2)}, u32[]{:S(2)}) async-start(bf16[128,24,128]{2,1,0:T(8,128)(2,1)} %bitcast.2), calls=%async_computation | async-start | bytes 1572864 | tf_op jit(solution)/shard_map/all_to_all | solution.py:239
  88.1 8.6 %collective-permute-start.1 = (bf16[38,152]{1,0:T(8,128)(2,1)S(1)}, bf16[38,152]{1,0:T(8,128)(2,1)S(1)}, u32[]{:S(2)}, u32[]{:S(2)}) collective-permute-start(bf16[38,152]{1,0:T(8,128)(2,1)S(1)} %get-tuple-element.23), channel_id=1, source_target_pairs={{0,1},{1,2},{2,3},{3,4},{4,5},{5,6},{6,7},{7,8},{8,9},{9,10},{10,1... | collective-permute-start | bytes 34664 | tf_op jit(solution)/shard_map/ppermute | solution.py:233

commit v4 on v3

--- a/solution.py
+++ b/solution.py
@@ -21,11 +21,12 @@
     return main,tail,mask,fold
 NACC=4
 CHUNK=64
-def fetch_operators(t_ref,t_buf,sems):
+def fetch_operators(ta_ref,tb_ref,t_buf,sems):
     copies=[]
     for q in range(5):
         n=min(CHUNK,NOPS-q*CHUNK)
-        copies.append(pltpu.make_async_copy(t_ref.at[pl.ds(q*CHUNK,n)],t_buf.at[pl.ds(q*CHUNK,n)],sems.at[q]))
+        source=ta_ref.at[pl.ds(q*CHUNK,n)] if q<4 else tb_ref
+        copies.append(pltpu.make_async_copy(source,t_buf.at[pl.ds(q*CHUNK,n)],sems.at[q]))
         copies[-1].start()
     return copies
 def translate_runs(places,src,dst,flip,copies,table,t_buf,xs,ys,accs):
@@ -71,8 +72,8 @@
 def widen(rows):
     up=rows.astype(f32)
     return up[:,:128],jnp.concatenate([up[:,128:],jnp.zeros((up.shape[0],104),f32)],axis=1)
-def backward_kernel(places,src,dst,up_ref,pm_ref,pt_ref,mask_ref,rep_ref,t_ref,local_ref,out_ref,t_buf,sems,table,xs,ys,*accs):
-    copies=fetch_operators(t_ref,t_buf,sems)
+def backward_kernel(places,src,dst,up_ref,pm_ref,pt_ref,mask_ref,rep_ref,ta_ref,tb_ref,local_ref,out_ref,t_buf,sems,table,xs,ys,*accs):
+    copies=fetch_operators(ta_ref,tb_ref,t_buf,sems)
     xs[...]=jnp.zeros_like(xs)
     ys[...]=jnp.zeros_like(ys)
     for acc in accs:
@@ -90,8 +91,8 @@
         out_ref[pl.ds(pl.multiple_of(192*g,192),192),:]=packed.astype(bf16)
         return 0
     lax.fori_loop(0,16,step,0,unroll=2)
-def forward_kernel(places,src,dst,up_ref,came_ref,pm_ref,pt_ref,mask_ref,fold_ref,t_ref,own_ref,t_buf,sems,table,xs,ys,*accs):
-    copies=fetch_operators(t_ref,t_buf,sems)
+def forward_kernel(places,src,dst,up_ref,came_ref,pm_ref,pt_ref,mask_ref,fold_ref,ta_ref,tb_ref,own_ref,t_buf,sems,table,xs,ys,*accs):
+    copies=fetch_operators(ta_ref,tb_ref,t_buf,sems)
     xs[...]=jnp.zeros_like(xs)
     ys[...]=jnp.zeros_like(ys)
     for acc in accs:
@@ -115,59 +116,50 @@
 def scratch(rows,acc_rows):
     return [pltpu.VMEM((NOPS,152,152),bf16),pltpu.SemaphoreType.DMA((5,)),pltpu.VMEM((rows,128),f32),pltpu.VMEM((GROUP,32,128),f32),pltpu.VMEM((GROUP,32,128),f32)]+[pltpu.VMEM((acc_rows,128),f32)]*NACC
 LIM=46*1024*1024
-ANY=pl.BlockSpec(memory_space=pl.ANY)
-def backward(places,src,dst,up,t):
+ANY=pl.BlockSpec(memory_space=pltpu.HBM)
+def backward(places,src,dst,up,ta,tb):
     main,tail,mask,fold=pack_maps()
     c=lambda a,d: jnp.asarray(a.astype(np.float32),d)
-    return pl.pallas_call(backward_kernel,in_specs=[SM]*3+[VM]*5+[ANY],out_specs=[VM,VM],
+    return pl.pallas_call(backward_kernel,in_specs=[SM]*3+[VM]*5+[ANY]*2,out_specs=[VM,VM],
         out_shape=[jax.ShapeDtypeStruct((64,152),f32),jax.ShapeDtypeStruct((3072,128),bf16)],
         scratch_shapes=scratch(128,5312),compiler_params=pltpu.CompilerParams(vmem_limit_bytes=LIM),name="backward")(
-        places,src,dst,up,c(main,bf16),c(tail,bf16),c(mask,f32),c(fold.T,bf16),t)
-def forward(places,src,dst,up,came,t):
+        places,src,dst,up,c(main,bf16),c(tail,bf16),c(mask,f32),c(fold.T,bf16),ta,tb)
+def forward(places,src,dst,up,came,ta,tb):
     main,tail,mask,fold=pack_maps()
     c=lambda a,d: jnp.asarray(a.astype(np.float32),d)
-    return pl.pallas_call(forward_kernel,in_specs=[SM]*3+[VM]*6+[ANY],out_specs=VM,
+    return pl.pallas_call(forward_kernel,in_specs=[SM]*3+[VM]*6+[ANY]*2,out_specs=VM,
         out_shape=jax.ShapeDtypeStruct((64,152),f32),
         scratch_shapes=scratch(5264,128),compiler_params=pltpu.CompilerParams(vmem_limit_bytes=LIM),name="forward")(
-        places,src,dst,up,came,c(main.T,bf16),c(tail.T,bf16),c(mask,f32),c(fold,bf16),t)
-def operator_kernel(m_ref,t_ref,s1,s2):
-    block=pl.program_id(0); part=pl.program_id(1)
-    def turn(n):
-        eye=(lax.broadcasted_iota(jnp.int32,(n,n),0)==lax.broadcasted_iota(jnp.int32,(n,n),1)).astype(bf16)
-        def body(g,_):
-            for u in range(19):
-                j=19*g+u
-                if u%3==2:
-                    t=lax.dot_general(eye,m_ref[j,:,0:n],(((1,),(1,)),((),())),preferred_element_type=f32)
-                else:
-                    t=m_ref[j,:,0:n].T.astype(f32)
-                s1[pl.ds(part*76+j,n,stride=153),:]=t[:,:128]
-                s2[pl.ds(part*76+j,n,stride=153),0:24]=t[:,128:]
-            return 0
-        lax.fori_loop(0,4,body,0)
-    def collect(n):
-        def body(q,_):
+        places,src,dst,up,came,c(main.T,bf16),c(tail.T,bf16),c(mask,f32),c(fold,bf16),ta,tb)
+def operator_kernel(n,m_ref,t_ref,s1,s2):
+    part=pl.program_id(1)
+    w=min(128,n+4)
+    eye=(lax.broadcasted_iota(jnp.int32,(w,w),0)==lax.broadcasted_iota(jnp.int32,(w,w),1)).astype(bf16)
+    def turn(g,_):
+        for u in range(19):
+            j=19*g+u
+            if u%3==2:
+                t=lax.dot_general(eye,m_ref[j,:,0:w],(((1,),(1,)),((),())),preferred_element_type=f32)
+            else:
+                t=m_ref[j,:,0:w].T.astype(f32)
+            s1[pl.ds(part*76+j,w,stride=153),:]=t[:,:128]
+            s2[pl.ds(part*76+j,w,stride=153),0:24]=t[:,128:]
+        return 0
+    lax.fori_loop(0,4,turn,0)
+    @pl.when(part==1)
+    def _():
+        def collect(q,_):
             for u in range(4):
                 k=4*q+u
                 t_ref[k,:,0:128]=s1[pl.ds(k*153,152),:].astype(bf16)
                 t_ref[k,:,128:152]=s2[pl.ds(k*153,152),:][:,:24].astype(bf16)
             return 0
-        lax.fori_loop(0,n//4,body,0)
-    @pl.when(block<2)
-    def _():
-        turn(128)
-    @pl.when(block==2)
-    def _():
-        turn(64)
-    @pl.when((part==1)&(block<2))
-    def _():
-        collect(128)
-    @pl.when((part==1)&(block==2))
-    def _():
-        collect(60)
-def operators(m):
-    return pl.pallas_call(operator_kernel,grid=(3,2),in_specs=[pl.BlockSpec((76,152,128),lambda i,j:(j,0,i))],
-      out_specs=pl.BlockSpec((128,152,152),lambda i,j:(i,0,0)),out_shape=jax.ShapeDtypeStruct((NOPS,152,152),bf16),
+        lax.fori_loop(0,n//4,collect,0)
+HEAD=256
+def operators(m,first,count,n):
+    return pl.pallas_call(functools.partial(operator_kernel,n),grid=(count,2),
+      in_specs=[pl.BlockSpec((76,152,128),lambda i,j:(j,0,i+first))],
+      out_specs=pl.BlockSpec((n,152,152),lambda i,j:(i,0,0)),out_shape=jax.ShapeDtypeStruct((count*n,152,152),bf16),
       scratch_shapes=[pltpu.VMEM((128*153,128),f32)]*2,
       compiler_params=pltpu.CompilerParams(vmem_limit_bytes=50*1024*1024),name="operators")(m)
 
@@ -239,18 +231,22 @@
     return lax.all_to_all(x.reshape(128,24,128),AXES,split_axis=0,concat_axis=0,tiled=True).reshape(3072,128)
 def shards(leaves, coarse_local, m2m, m2l, c2e, l2l, send_box, pair_box, pair_partner, pair_op):
     width=152; box_count=64; edge=EDGE
-    ops=operators(jnp.transpose(m2l,(1,2,0)))
-    front_sum,own_sum=gather_children(leaves.T,m2m)
+    m2l_t=jnp.transpose(m2l,(1,2,0))
+    ops_a=operators(m2l_t,0,2,128)
+    leaves_t,m2m,ops_a=lax.optimization_barrier((leaves.T,m2m,ops_a))
+    front_sum,own_sum=gather_children(leaves_t,m2m)
     arrived=shifted(front_sum,-1)
+    front_sum,own_sum,m2l_t=lax.optimization_barrier((front_sum,own_sum,m2l_t))
+    ops_b=operators(m2l_t,2,1,60)
     places=run_places(pair_op.reshape(NOPS,OPCAP)[:,0])
     partner=pad_to(2*jnp.where(pair_partner>=0,pair_partner,2624),SLOTS,2*2624)
     box=pad_to(2*pair_box,SLOTS,0)
-    arrived,ops=lax.optimization_barrier((arrived,ops))
+    arrived,ops_b=lax.optimization_barrier((arrived,ops_b))
     packed,up,index=pack_sends(send_box,own_sum,arrived)
     came=exchange(packed)
-    local,to_owners=backward(places,box,partner,up,ops)
+    local,to_owners=backward(places,box,partner,up,ops_a,ops_b)
     returned=exchange(to_owners)
-    own=forward(places,partner,box,up,came,ops)
+    own=forward(places,partner,box,up,came,ops_a,ops_b)
     parent,edges=finish(index,returned,local,own,c2e,coarse_local)
     earlier=shifted(edges,1)
     head=jnp.einsum("pj,oji->poi",earlier,l2l,preferred_element_type=f32).reshape(8*edge,width)

time: 98.2 us -> 102 us (1.039)
  Pallas kernels: 59.3 us -> 62.4 us
  local copies, waits for them, and re-layouts: 3.82 us -> 6.43 us
  waiting for transfers between devices: 8.02 us -> 6.52 us
    pallas_call x3 -> x4, Pallas kernels: 54.2 us -> 57.3 us  [the longest x2 24 us: operators(): pl.pallas_call(functools.partial(operator_kernel, n), grid=(count, 2), in...]
    unnamed x31 -> x37, local copies, waits for them, and re-layouts: 3.01 us -> 5.61 us
    all_to_all x2, waiting for transfers between devices: 1.37 us -> 0.01 us  [exchange(): lax.all_to_all(x.reshape(128, 24, 128), AXES, split_axis=0, concat_axis=0...]
  transfers between devices with their start and end apart: 4 -> 4, of which waited for: 2 -> 1; matrix products, arithmetic and copies ran while one was open for 3% -> 2% of each run, Pallas kernels for 55% -> 40%
where the time goes in v4:
time: 102 us
  Pallas kernels  62.4 us (61%)
  starting transfers between devices  23.7 us (23%)
  waiting for transfers between devices  6.52 us (6%)
  local copies, waits for them, and re-layouts  6.43 us (6%)
  matrix products  1.21 us (1%)
    pallas_call x2, Pallas kernels, operators(): pl.pallas_call(functools.partial(operator_kernel, n), grid=(count, 2), in...  24 us
    pallas_call x1, Pallas kernels, backward(): pl.pallas_call(backward_kernel, in_specs=[SM] * 3 + [VM] * 5 + [ANY] * 2,...  18.3 us
    pallas_call x1, Pallas kernels, forward(): pl.pallas_call(forward_kernel, in_specs=[SM] * 3 + [VM] * 6 + [ANY] * 2,...  15 us
    all_to_all x2, starting transfers between devices, exchange(): lax.all_to_all(x.reshape(128, 24, 128), AXES, split_axis=0, concat_axis=0...  14.7 us
    ppermute x2, starting transfers between devices, shifted(): return lax.ppermute(x, AXES, [(i, (i + by) % count) for i in range(count)])  9.06 us
    ppermute x2, waiting for transfers between devices, shifted(): return lax.ppermute(x, AXES, [(i, (i + by) % count) for i in range(count)])  6.51 us
    unnamed x37, local copies, waits for them, and re-layouts  5.61 us
    pallas_call x1, Pallas kernels, pack_sends(): pl.pallas_call(send_kernel, in_specs=[VM] * 6, out_specs=[VM] * 3, out_sh...  2.21 us
  transfers between devices with their start and end apart: 4, of which 1 were waited for; matrix products, arithmetic and copies ran while one was open for 2% of the time, Pallas kernels for 40%

profile of v4, /device:TPU:0, one launch (start us, length us, event | category | flops | bytes accessed | tf_op | source)
XLA Modules:
  0.0 101.6 jit_solution(1950679483114700449)
XLA Ops:
  0.6 0.0 copy-start
  0.6 0.0 copy-start.3
  0.7 0.0 copy-start.7
  0.7 0.0 copy-start.15
  0.7 16.9 %operators.2.ta_ref = bf16[256,152,152]{2,1,0:T(8,128)(2,1)} custom-call(bf16[152,152,316]{2,1,0:T(8,128)(2,1)} %bitcast.23), custom_call_target="tpu_custom_call" | custom-call | tf_op jit(solution)/shard_map/operators/pallas_call | solution.py:160
  17.6 0.0 copy-start.14
  17.6 0.0 copy-start.16
  17.6 0.0 copy-start.4
  17.7 0.0 copy-start.10
  17.7 0.0 copy-start.11
  17.7 0.0 copy-done.3
  17.7 0.0 copy-done.7
  17.7 1.0 gather.1
  18.7 8.3 %collective-permute-start = (f32[38,152]{1,0:T(8,128)S(1)}, f32[38,152]{1,0:T(8,128)S(1)}, u32[]{:S(2)}, u32[]{:S(2)}) collective-permute-start(f32[38,152]{1,0:T(8,128)S(1)} %get-tuple-element.20), channel_id=1, source_target_pairs={{0,127},{1,0},{2,1},{3,2},{4,3},{5,4},{6,5},{7,6},{8,7},{9,8},{10,... | collective-permute-start | bytes 69320 | tf_op jit(solution)/shard_map/ppermute | solution.py:225
  26.9 0.0 copy-done.15
  27.0 7.1 %operators.3.tb_ref = bf16[60,152,152]{2,1,0:T(8,128)(2,1)} custom-call(bf16[152,152,316]{2,1,0:T(8,128)(2,1)} %bitcast.24), custom_call_target="tpu_custom_call" | custom-call | tf_op jit(solution)/shard_map/operators/pallas_call | solution.py:160
  34.0 0.0 copy-done.17
  34.0 0.2 reshape.31
  34.2 0.0 collective-permute-done.arrived_ref
  34.2 0.0 copy-done.5
  34.2 0.0 copy-done.6
  34.3 0.0 copy-done.9
  34.3 0.0 copy-done.14
  34.3 2.2 %send.1 = (bf16[3072,128]{1,0:T(8,128)(2,1)}, bf16[64,152]{1,0:T(8,128)(2,1)S(1)}, f32[96,192]{1,0:T(8,128)S(1)}) custom-call(s32[1,2560]{1,0:T(1,128)S(1)} %copy-done.14, f32[64,152]{1,0:T(8,128)S(1)} %get-tuple-element.22.own_ref, f32[38,152]{1,0:T(8,128)S(1)} %collective-permute-done.arrived_ref, bf16[160,192]{1,0:T(8,128)(2,1)S(1)} %copy-done.5, ...), custom_call_target="tpu_custom_call" | custom-call | tf_op jit(solution)/shard_map/send/pallas_call | solution.py:202
  36.5 4.6 %all-to-all-start.1 = ((bf16[128,24,128]{2,1,0:T(8,128)(2,1)}), bf16[128,24,128]{2,1,0:T(8,128)(2,1)S(1)}, u32[]{:S(2)}, u32[]{:S(2)}) async-start(bf16[128,24,128]{2,1,0:T(8,128)(2,1)} %bitcast.4), calls=%async_computation.1 | async-start | bytes 1572864 | tf_op jit(solution)/shard_map/all_to_all | solution.py:231
  41.1 0.1 slice_reduce_fusion
  41.3 0.0 copy-done.16
  41.3 0.2 select_reduce_fusion
  41.5 0.0 copy-done.4
  41.5 2.3 %copy-done.1 = bf16[60,152,152]{2,1,0:T(8,128)(2,1)S(1)} copy-done((bf16[60,152,152]{2,1,0:T(8,128)(2,1)S(1)}, bf16[60,152,152]{2,1,0:T(8,128)(2,1)}, u32[]{:S(2)}) %copy-start.1) | copy-done | bytes 2772504
  43.8 18.3 %backward.1 = (f32[64,152]{1,0:T(8,128)S(1)}, bf16[3072,128]{1,0:T(8,128)(2,1)}) custom-call(s32[320]{0:T(512)S(1)} %fusion.5.places, s32[4160]{0:T(1024)S(1)} %concatenate.13.src.dst, s32[4160]{0:T(1024)S(1)} %concatenate.14.dst.src, bf16[64,152]{1,0:T(8,128)(2,1)S(1)} %get-tuple-element.26.up_ref, bf16[192,160]{1,0:T(8,128)(2,1)S(1)} %copy-done.10, ...), custom_call_target="tpu_custom_call" | custom-call | tf_op jit(solution)/shard_map/backward/pallas_call | solution.py:123
  62.2 0.0 copy-start.8
  62.2 0.0 copy-start.13
  62.2 0.0 all-to-all-done.1
  62.2 10.1 %all-to-all-start = ((bf16[128,24,128]{2,1,0:T(8,128)(2,1)}), bf16[128,24,128]{2,1,0:T(8,128)(2,1)S(1)}, u32[]{:S(2)}, u32[]{:S(2)}) async-start(bf16[128,24,128]{2,1,0:T(8,128)(2,1)} %bitcast.2), calls=%async_computation | async-start | bytes 1572864 | tf_op jit(solution)/shard_map/all_to_all | solution.py:231
  72.3 0.0 copy-done.12
  72.3 0.0 copy-start.2
  72.3 2.3 %copy-done.2 = bf16[60,152,152]{2,1,0:T(8,128)(2,1)S(1)} copy-done((bf16[60,152,152]{2,1,0:T(8,128)(2,1)S(1)}, bf16[60,152,152]{2,1,0:T(8,128)(2,1)}, u32[]{:S(2)}) %copy-start.2) | copy-done | bytes 2772504
  74.6 15.0 %forward.1.own_ref = f32[64,152]{1,0:T(8,128)S(1)} custom-call(s32[320]{0:T(512)S(1)} %fusion.5.places, s32[4160]{0:T(1024)S(1)} %concatenate.14.dst.src, s32[4160]{0:T(1024)S(1)} %concatenate.13.src.dst, bf16[64,152]{1,0:T(8,128)(2,1)S(1)} %get-tuple-element.26.up_ref, bf16[3072,128]{1,0:T(8,128)(2,1)S(1)} %bitcast.20, bf16[160,192]{1,0:T(8,128)(2,1)S(1)} %copy-done.5, ...), custom_call_target="tpu_custom_call" | custom-call | tf_op jit(solution)/shard_map/forward/pallas_call | solution.py:130
  89.6 0.0 all-to-all-done
  89.7 1.9 %finish.1 = (bf16[64,152]{1,0:T(8,128)(2,1)}, bf16[38,152]{1,0:T(8,128)(2,1)S(1)}) custom-call(f32[96,192]{1,0:T(8,128)S(1)} %get-tuple-element.25.index_ref, bf16[3072,128]{1,0:T(8,128)(2,1)S(1)} %bitcast.21, f32[64,152]{1,0:T(8,128)S(1)} %get-tuple-element.30.local_ref, f32[64,152]{1,0:T(8,128)S(1)} %forward.1.own_ref, f32[152,152]{1,0:T(8,128)S(1)} %copy-done.8, ...), custom_call_target="tpu_custom_call" | custom-call | tf_op jit(solution)/shard_map/finish/pallas_call | solution.py:217
  91.6 0.8 collective-permute-start.1
  92.4 1.0 fusion
  93.4 0.3 copy.31
  93.7 6.5 %collective-permute-done.1 = bf16[38,152]{1,0:T(8,128)(2,1)S(1)} collective-permute-done((bf16[38,152]{1,0:T(8,128)(2,1)S(1)}, bf16[38,152]{1,0:T(8,128)(2,1)S(1)}, u32[]{:S(2)}, u32[]{:S(2)}) %collective-permute-start.1) | collective-permute-done | bytes 11584 | tf_op jit(solution)/shard_map/ppermute | solution.py:225
  100.3 0.2 fusion.3
  100.5 0.1 copy.32
  100.7 0.9 copy.28
  (21 shorter events, 0.1 us)
Async XLA Ops:
  0.6 91.8 %copy-start = (bf16[8,152,152]{2,1,0:T(8,128)(2,1)S(1)}, bf16[8,152,152]{2,1,0:T(8,128)(2,1)}, u32[]{:S(2)}) copy-start(bf16[8,152,152]{2,1,0:T(8,128)(2,1)} %param.26) | copy-start | bytes 1108996
  0.6 17.0 %copy-start.3 = (bf16[8,152,152]{2,1,0:T(8,128)(2,1)S(1)}, bf16[8,152,152]{2,1,0:T(8,128)(2,1)}, u32[]{:S(2)}) copy-start(bf16[8,152,152]{2,1,0:T(8,128)(2,1)} %m2m_ref) | copy-start | bytes 1108996
  0.7 17.0 %copy-start.7 = (bf16[512,152]{0,1:T(8,128)(2,1)S(1)}, bf16[512,152]{0,1:T(8,128)(2,1)}, u32[]{:S(2)}) copy-start(bf16[512,152]{0,1:T(8,128)(2,1)} %param.21) | copy-start | bytes 466948
  0.7 26.3 %copy-start.15 = (s32[4108]{0:T(1024)S(1)}, s32[4108]{0:T(1024)}, u32[]{:S(2)}) copy-start(s32[4108]{0:T(1024)} %param.28) | copy-start | bytes 49300
  17.6 16.4 %copy-start.17 = (s32[4108]{0:T(1024)S(1)}, s32[4108]{0:T(1024)}, u32[]{:S(2)}) copy-start(s32[4108]{0:T(1024)} %param.30) | copy-start | bytes 49300
  17.6 16.6 %copy-start.5 = (bf16[160,192]{1,0:T(8,128)(2,1)S(1)}, bf16[160,192]{1,0:T(8,128)(2,1)}, u32[]{:S(2)}) copy-start(bf16[160,192]{1,0:T(8,128)(2,1)} %constant.11.clone.pm_ref) | copy-start | bytes 184324
  17.6 16.6 %copy-start.6 = (bf16[160,192]{1,0:T(8,128)(2,1)S(1)}, bf16[160,192]{1,0:T(8,128)(2,1)}, u32[]{:S(2)}) copy-start(bf16[160,192]{1,0:T(8,128)(2,1)} %constant.12.clone.pt_ref) | copy-start | bytes 184324
  17.6 16.6 %copy-start.9 = (bf16[128,128]{1,0:T(8,128)(2,1)S(1)}, bf16[128,128]{1,0:T(8,128)(2,1)}, u32[]{:S(2)}) copy-start(bf16[128,128]{1,0:T(8,128)(2,1)} %constant.13.clone.rep_ref) | copy-start | bytes 98308
  17.6 16.6 %copy-start.14 = (s32[1,2560]{1,0:T(1,128)S(1)}, s32[1,2560]{1,0:T(1,128)}, u32[]{:S(2)}) copy-start(s32[1,2560]{1,0:T(1,128)} %send_ref.1) | copy-start | bytes 30724
  17.6 23.6 %copy-start.16 = (s32[4108]{0:T(1024)S(1)}, s32[4108]{0:T(1024)}, u32[]{:S(2)}) copy-start(s32[4108]{0:T(1024)} %param.29) | copy-start | bytes 49300
  17.6 23.8 %copy-start.4 = (f32[160,128]{1,0:T(8,128)S(1)}, f32[160,128]{1,0:T(8,128)}, u32[]{:S(2)}) copy-start(f32[160,128]{1,0:T(8,128)} %constant.36.clone.mask_ref) | copy-start | bytes 245764
  17.7 23.8 %copy-start.10 = (bf16[192,160]{1,0:T(8,128)(2,1)S(1)}, bf16[192,160]{1,0:T(8,128)(2,1)}, u32[]{:S(2)}) copy-start(bf16[192,160]{1,0:T(8,128)(2,1)} %constant.34.clone.pm_ref) | copy-start | bytes 184324
  17.7 23.8 %copy-start.11 = (bf16[192,160]{1,0:T(8,128)(2,1)S(1)}, bf16[192,160]{1,0:T(8,128)(2,1)}, u32[]{:S(2)}) copy-start(bf16[192,160]{1,0:T(8,128)(2,1)} %constant.35.clone.pt_ref) | copy-start | bytes 184324
  18.7 15.6 %collective-permute-start = (f32[38,152]{1,0:T(8,128)S(1)}, f32[38,152]{1,0:T(8,128)S(1)}, u32[]{:S(2)}, u32[]{:S(2)}) collective-permute-start(f32[38,152]{1,0:T(8,128)S(1)} %get-tuple-element.20), channel_id=1, source_target_pairs={{0,127},{1,0},{2,1},{3,2},{4,3},{5,4},{6,5},{7,6},{8,7},{9,8},{10,... | collective-permute-start | bytes 69320 | tf_op jit(solution)/shard_map/ppermute | solution.py:225
  34.0 38.3 %copy-start.12 = (bf16[128,128]{1,0:T(8,128)(2,1)S(1)}, bf16[128,128]{1,0:T(8,128)(2,1)}, u32[]{:S(2)}) copy-start(bf16[128,128]{1,0:T(8,128)(2,1)} %constant.37.clone.fold_ref) | copy-start | bytes 98308
  36.5 25.7 %all-to-all-start.1 = ((bf16[128,24,128]{2,1,0:T(8,128)(2,1)}), bf16[128,24,128]{2,1,0:T(8,128)(2,1)S(1)}, u32[]{:S(2)}, u32[]{:S(2)}) async-start(bf16[128,24,128]{2,1,0:T(8,128)(2,1)} %bitcast.4), calls=%async_computation.1 | async-start | bytes 1572864 | tf_op jit(solution)/shard_map/all_to_all | solution.py:231
  41.5 2.3 %copy-start.1 = (bf16[60,152,152]{2,1,0:T(8,128)(2,1)S(1)}, bf16[60,152,152]{2,1,0:T(8,128)(2,1)}, u32[]{:S(2)}) copy-start(bf16[60,152,152]{2,1,0:T(8,128)(2,1)} %operators.3.tb_ref) | copy-start | bytes 8317444
  62.2 27.5 %copy-start.8 = (f32[152,152]{1,0:T(8,128)S(1)}, f32[152,152]{1,0:T(8,128)}, u32[]{:S(2)}) copy-start(f32[152,152]{1,0:T(8,128)} %c2e_ref.1) | copy-start | bytes 277252
  62.2 27.5 %copy-start.13 = (bf16[64,152]{1,0:T(8,128)(2,1)S(1)}, bf16[64,152]{1,0:T(8,128)(2,1)}, u32[]{:S(2)}) copy-start(bf16[64,152]{1,0:T(8,128)(2,1)} %coarse_ref.1) | copy-start | bytes 58372
  62.2 27.5 %all-to-all-start = ((bf16[128,24,128]{2,1,0:T(8,128)(2,1)}), bf16[128,24,128]{2,1,0:T(8,128)(2,1)S(1)}, u32[]{:S(2)}, u32[]{:S(2)}) async-start(bf16[128,24,128]{2,1,0:T(8,128)(2,1)} %bitcast.2), calls=%async_computation | async-start | bytes 1572864 | tf_op jit(solution)/shard_map/all_to_all | solution.py:231
  72.3 2.3 %copy-start.2 = (bf16[60,152,152]{2,1,0:T(8,128)(2,1)S(1)}, bf16[60,152,152]{2,1,0:T(8,128)(2,1)}, u32[]{:S(2)}) copy-start(bf16[60,152,152]{2,1,0:T(8,128)(2,1)} %operators.3.tb_ref) | copy-start | bytes 8317444
  91.6 8.6 %collective-permute-start.1 = (bf16[38,152]{1,0:T(8,128)(2,1)S(1)}, bf16[38,152]{1,0:T(8,128)(2,1)S(1)}, u32[]{:S(2)}, u32[]{:S(2)}) collective-permute-start(bf16[38,152]{1,0:T(8,128)(2,1)S(1)} %get-tuple-element.33), channel_id=1, source_target_pairs={{0,1},{1,2},{2,3},{3,4},{4,5},{5,6},{6,7},{7,8},{8,9},{9,10},{10,1... | collective-permute-start | bytes 34664 | tf_op jit(solution)/shard_map/ppermute | solution.py:225

commit v5 on v3

--- a/solution.py
+++ b/solution.py
@@ -9,7 +9,7 @@
 from jax.sharding import PartitionSpec as P
 f32=jnp.float32; bf16=jnp.bfloat16
 NOPS=316; CAP=20; LEAD=300; OPCAP=13
-RUNS=320; SLOTS=4160; COLS=4224; GROUP=32
+RUNS=320; SLOTS=4160; COLS=4224; GROUP=64
 def pack_maps():
     row=np.arange(192)[:,None]; col=np.arange(160)[None,:]
     same=row//24==col//20
@@ -89,7 +89,7 @@
         packed=jnp.dot(pm_ref[...],main.astype(bf16),preferred_element_type=f32)+jnp.dot(pt_ref[...],tail,preferred_element_type=f32)
         out_ref[pl.ds(pl.multiple_of(192*g,192),192),:]=packed.astype(bf16)
         return 0
-    lax.fori_loop(0,16,step,0,unroll=2)
+    lax.fori_loop(0,16,step,0,unroll=8)
 def forward_kernel(places,src,dst,up_ref,came_ref,pm_ref,pt_ref,mask_ref,fold_ref,t_ref,own_ref,t_buf,sems,table,xs,ys,*accs):
     copies=fetch_operators(t_ref,t_buf,sems)
     xs[...]=jnp.zeros_like(xs)
@@ -106,7 +106,7 @@
         tail=jnp.dot(tail,fold_ref[...],preferred_element_type=f32)
         store_rows(table,128+320*g,main,tail)
         return 0
-    lax.fori_loop(0,16,unpack,0,unroll=4)
+    lax.fori_loop(0,16,unpack,0,unroll=8)
     translate_runs(places,src,dst,False,copies,table,t_buf,xs,ys,accs)
     m,t=sum_rows(accs,0,64)
     own_ref[:,:128]=m

time: 98.2 us -> 96.4 us (0.982)
  Pallas kernels: 59.3 us -> 56.4 us
    pallas_call x1, Pallas kernels: 18.3 us -> 16.3 us  [backward(): pl.pallas_call(backward_kernel, in_specs=[SM] * 3 + [VM] * 5 + [ANY], out...]
  transfers between devices with their start and end apart: 4 -> 4, of which waited for: 2 -> 2; matrix products, arithmetic and copies ran while one was open for 3% -> 3% of each run, Pallas kernels for 55% -> 53%
where the time goes in v5:
time: 96.4 us; the launch traced here: 96.1 us
  Pallas kernels  56.4 us (59%)
  starting transfers between devices  23.9 us (25%)
  waiting for transfers between devices  8.88 us (9%)
  local copies, waits for them, and re-layouts  3.82 us (4%)
  matrix products  1.21 us (1%)
    pallas_call x1, Pallas kernels, operators(): pl.pallas_call(operator_kernel, grid=(3, 2), in_specs=[pl.BlockSpec((76,...  21.5 us
    pallas_call x1, Pallas kernels, backward(): pl.pallas_call(backward_kernel, in_specs=[SM] * 3 + [VM] * 5 + [ANY], out...  16.3 us
    all_to_all x2, starting transfers between devices, exchange(): lax.all_to_all(x.reshape(128, 24, 128), AXES, split_axis=0, concat_axis=0...  14.9 us
    pallas_call x1, Pallas kernels, forward(): pl.pallas_call(forward_kernel, in_specs=[SM] * 3 + [VM] * 6 + [ANY], out_...  13.5 us
    ppermute x2, starting transfers between devices, shifted(): return lax.ppermute(x, AXES, [(i, (i + by) % count) for i in range(count)])  8.91 us
    ppermute x2, waiting for transfers between devices, shifted(): return lax.ppermute(x, AXES, [(i, (i + by) % count) for i in range(count)])  6.66 us
    unnamed x31, local copies, waits for them, and re-layouts  3.01 us
    all_to_all x2, waiting for transfers between devices, exchange(): lax.all_to_all(x.reshape(128, 24, 128), AXES, split_axis=0, concat_axis=0...  2.23 us
  transfers between devices with their start and end apart: 4, of which 2 were waited for; matrix products, arithmetic and copies ran while one was open for 3% of the time, Pallas kernels for 53%

profile of v5, /device:TPU:0, one launch (start us, length us, event | category | flops | bytes accessed | tf_op | source)
XLA Modules:
  0.0 96.1 jit_solution(13143886410146038132)
XLA Ops:
  0.6 0.0 copy-start
  0.6 0.0 copy-start.1
  0.7 1.1 %copy-done.1 = bf16[8,152,152]{2,1,0:T(8,128)(2,1)S(1)} copy-done((bf16[8,152,152]{2,1,0:T(8,128)(2,1)S(1)}, bf16[8,152,152]{2,1,0:T(8,128)(2,1)}, u32[]{:S(2)}) %copy-start.1) | copy-done | bytes 369688
  1.8 0.0 copy-start.5
  1.8 0.9 copy-done.5
  2.7 0.0 copy-start.12
  2.7 0.0 copy-start.13
  2.7 0.0 copy-start.2
  2.7 0.0 copy-start.8
  2.8 0.0 copy-start.9
  2.8 1.0 gather.1
  3.7 8.3 %collective-permute-start = (f32[38,152]{1,0:T(8,128)S(1)}, f32[38,152]{1,0:T(8,128)S(1)}, u32[]{:S(2)}, u32[]{:S(2)}) collective-permute-start(f32[38,152]{1,0:T(8,128)S(1)} %get-tuple-element.14), channel_id=1, source_target_pairs={{0,127},{1,0},{2,1},{3,2},{4,3},{5,4},{6,5},{7,6},{8,7},{9,8},{10,... | collective-permute-start | bytes 69320 | tf_op jit(solution)/shard_map/ppermute | solution.py:233
  12.0 0.7 broadcast_multiply_fusion
  12.7 21.5 %operators.1.t_ref = bf16[316,152,152]{2,1,0:T(8,128)(2,1)} custom-call(bf16[152,152,316]{2,1,0:T(8,128)(2,1)} %bitcast.23), custom_call_target="tpu_custom_call" | custom-call | tf_op jit(solution)/shard_map/operators/pallas_call | solution.py:169
  34.2 0.0 copy-done.14
  34.2 0.2 reshape.31
  34.4 0.0 collective-permute-done.arrived_ref
  34.4 0.0 copy-done.3
  34.4 0.0 copy-done.4
  34.4 0.0 copy-done.7
  34.5 0.0 copy-done.12
  34.5 2.2 %send.1 = (bf16[3072,128]{1,0:T(8,128)(2,1)}, bf16[64,152]{1,0:T(8,128)(2,1)S(1)}, f32[96,192]{1,0:T(8,128)S(1)}) custom-call(s32[1,2560]{1,0:T(1,128)S(1)} %copy-done.12, f32[64,152]{1,0:T(8,128)S(1)} %get-tuple-element.13.own_ref, f32[38,152]{1,0:T(8,128)S(1)} %collective-permute-done.arrived_ref, bf16[160,192]{1,0:T(8,128)(2,1)S(1)} %copy-done.3, ...), custom_call_target="tpu_custom_call" | custom-call | tf_op jit(solution)/shard_map/send/pallas_call | solution.py:210
  36.7 4.8 %all-to-all-start.1 = ((bf16[128,24,128]{2,1,0:T(8,128)(2,1)}), bf16[128,24,128]{2,1,0:T(8,128)(2,1)S(1)}, u32[]{:S(2)}, u32[]{:S(2)}) async-start(bf16[128,24,128]{2,1,0:T(8,128)(2,1)} %bitcast.4), calls=%async_computation.1 | async-start | bytes 1572864 | tf_op jit(solution)/shard_map/all_to_all | solution.py:239
  41.5 0.1 slice_reduce_fusion
  41.7 0.0 copy-done.13
  41.7 0.2 select_reduce_fusion
  41.9 0.0 copy-done.2
  41.9 0.0 copy-done.8
  41.9 0.0 copy-done.9
  41.9 0.0 copy-start.6
  41.9 0.0 copy-start.11
  41.9 16.3 %backward.1 = (f32[64,152]{1,0:T(8,128)S(1)}, bf16[3072,128]{1,0:T(8,128)(2,1)}) custom-call(s32[320]{0:T(512)S(1)} %fusion.5.places, s32[4160]{0:T(1024)S(1)} %concatenate.13.src.dst, s32[4160]{0:T(1024)S(1)} %concatenate.14.dst.src, bf16[64,152]{1,0:T(8,128)(2,1)S(1)} %get-tuple-element.17.up_ref, bf16[192,160]{1,0:T(8,128)(2,1)S(1)} %copy-done.8, ...), custom_call_target="tpu_custom_call" | custom-call | tf_op jit(solution)/shard_map/backward/pallas_call | solution.py:122
  58.3 0.0 all-to-all-done.1
  58.3 10.1 %all-to-all-start = ((bf16[128,24,128]{2,1,0:T(8,128)(2,1)}), bf16[128,24,128]{2,1,0:T(8,128)(2,1)S(1)}, u32[]{:S(2)}, u32[]{:S(2)}) async-start(bf16[128,24,128]{2,1,0:T(8,128)(2,1)} %bitcast.2), calls=%async_computation | async-start | bytes 1572864 | tf_op jit(solution)/shard_map/all_to_all | solution.py:239
  68.4 0.0 copy-done.10
  68.4 13.5 %forward.1.own_ref = f32[64,152]{1,0:T(8,128)S(1)} custom-call(s32[320]{0:T(512)S(1)} %fusion.5.places, s32[4160]{0:T(1024)S(1)} %concatenate.14.dst.src, s32[4160]{0:T(1024)S(1)} %concatenate.13.src.dst, bf16[64,152]{1,0:T(8,128)(2,1)S(1)} %get-tuple-element.17.up_ref, bf16[3072,128]{1,0:T(8,128)(2,1)S(1)} %bitcast.20, bf16[160,192]{1,0:T(8,128)(2,1)S(1)} %copy-done.3, ...), custom_call_target="tpu_custom_call" | custom-call | tf_op jit(solution)/shard_map/forward/pallas_call | solution.py:129
  82.0 2.2 %all-to-all-done = bf16[128,24,128]{2,1,0:T(8,128)(2,1)S(1)} async-done(((bf16[128,24,128]{2,1,0:T(8,128)(2,1)}), bf16[128,24,128]{2,1,0:T(8,128)(2,1)S(1)}, u32[]{:S(2)}, u32[]{:S(2)}) %all-to-all-start) | async-done | bytes 786464 | tf_op jit(solution)/shard_map/all_to_all | solution.py:239
  84.2 0.0 copy-done.6
  84.2 0.0 copy-done.11
  84.2 1.9 %finish.1 = (bf16[64,152]{1,0:T(8,128)(2,1)}, bf16[38,152]{1,0:T(8,128)(2,1)S(1)}) custom-call(f32[96,192]{1,0:T(8,128)S(1)} %get-tuple-element.16.index_ref, bf16[3072,128]{1,0:T(8,128)(2,1)S(1)} %bitcast.21, f32[64,152]{1,0:T(8,128)S(1)} %get-tuple-element.20.local_ref, f32[64,152]{1,0:T(8,128)S(1)} %forward.1.own_ref, f32[152,152]{1,0:T(8,128)S(1)} %copy-done.6, ...), custom_call_target="tpu_custom_call" | custom-call | tf_op jit(solution)/shard_map/finish/pallas_call | solution.py:225
  86.1 0.6 collective-permute-start.1
  86.8 0.0 copy-done
  86.8 1.0 %fusion = f32[64,8,152]{2,0,1:T(8,128)S(1)} fusion(bf16[8,152,152]{2,1,0:T(8,128)(2,1)S(1)} %copy-done, bf16[64,152]{1,0:T(8,128)(2,1)} %get-tuple-element.26), kind=kOutput, calls=%fused_computation.7 | convolution fusion | flops 23658496 | bytes 700416 | tf_op jit(solution)/shard_map/pj,oji->poi/dot_general | solution.py:257
  87.8 0.3 copy.31
  88.1 6.7 %collective-permute-done.1 = bf16[38,152]{1,0:T(8,128)(2,1)S(1)} collective-permute-done((bf16[38,152]{1,0:T(8,128)(2,1)S(1)}, bf16[38,152]{1,0:T(8,128)(2,1)S(1)}, u32[]{:S(2)}, u32[]{:S(2)}) %collective-permute-start.1) | collective-permute-done | bytes 11584 | tf_op jit(solution)/shard_map/ppermute | solution.py:233
  94.8 0.2 fusion.3
  95.0 0.1 copy.32
  95.2 0.9 copy.28
  (14 shorter events, 0.1 us)
Async XLA Ops:
  0.6 86.1 %copy-start = (bf16[8,152,152]{2,1,0:T(8,128)(2,1)S(1)}, bf16[8,152,152]{2,1,0:T(8,128)(2,1)}, u32[]{:S(2)}) copy-start(bf16[8,152,152]{2,1,0:T(8,128)(2,1)} %param.26) | copy-start | bytes 1108996
  0.6 1.1 %copy-start.1 = (bf16[8,152,152]{2,1,0:T(8,128)(2,1)S(1)}, bf16[8,152,152]{2,1,0:T(8,128)(2,1)}, u32[]{:S(2)}) copy-start(bf16[8,152,152]{2,1,0:T(8,128)(2,1)} %m2m_ref.1) | copy-start | bytes 1108996
  1.8 0.9 copy-start.5
  2.7 31.5 %copy-start.14 = (s32[4108]{0:T(1024)S(1)}, s32[4108]{0:T(1024)}, u32[]{:S(2)}) copy-start(s32[4108]{0:T(1024)} %param.30) | copy-start | bytes 49300
  2.7 31.7 %copy-start.3 = (bf16[160,192]{1,0:T(8,128)(2,1)S(1)}, bf16[160,192]{1,0:T(8,128)(2,1)}, u32[]{:S(2)}) copy-start(bf16[160,192]{1,0:T(8,128)(2,1)} %constant.11.clone.pm_ref) | copy-start | bytes 184324
  2.7 31.7 %copy-start.4 = (bf16[160,192]{1,0:T(8,128)(2,1)S(1)}, bf16[160,192]{1,0:T(8,128)(2,1)}, u32[]{:S(2)}) copy-start(bf16[160,192]{1,0:T(8,128)(2,1)} %constant.12.clone.pt_ref) | copy-start | bytes 184324
  2.7 31.7 %copy-start.7 = (bf16[128,128]{1,0:T(8,128)(2,1)S(1)}, bf16[128,128]{1,0:T(8,128)(2,1)}, u32[]{:S(2)}) copy-start(bf16[128,128]{1,0:T(8,128)(2,1)} %constant.13.clone.rep_ref) | copy-start | bytes 98308
  2.7 31.7 %copy-start.12 = (s32[1,2560]{1,0:T(1,128)S(1)}, s32[1,2560]{1,0:T(1,128)}, u32[]{:S(2)}) copy-start(s32[1,2560]{1,0:T(1,128)} %send_ref.1) | copy-start | bytes 30724
  2.7 38.9 %copy-start.13 = (s32[4108]{0:T(1024)S(1)}, s32[4108]{0:T(1024)}, u32[]{:S(2)}) copy-start(s32[4108]{0:T(1024)} %param.29) | copy-start | bytes 49300
  2.7 39.1 %copy-start.2 = (f32[160,128]{1,0:T(8,128)S(1)}, f32[160,128]{1,0:T(8,128)}, u32[]{:S(2)}) copy-start(f32[160,128]{1,0:T(8,128)} %constant.36.clone.mask_ref) | copy-start | bytes 245764
  2.7 39.1 %copy-start.8 = (bf16[192,160]{1,0:T(8,128)(2,1)S(1)}, bf16[192,160]{1,0:T(8,128)(2,1)}, u32[]{:S(2)}) copy-start(bf16[192,160]{1,0:T(8,128)(2,1)} %constant.34.clone.pm_ref) | copy-start | bytes 184324
  2.8 39.1 %copy-start.9 = (bf16[192,160]{1,0:T(8,128)(2,1)S(1)}, bf16[192,160]{1,0:T(8,128)(2,1)}, u32[]{:S(2)}) copy-start(bf16[192,160]{1,0:T(8,128)(2,1)} %constant.35.clone.pt_ref) | copy-start | bytes 184324
  3.7 30.7 %collective-permute-start = (f32[38,152]{1,0:T(8,128)S(1)}, f32[38,152]{1,0:T(8,128)S(1)}, u32[]{:S(2)}, u32[]{:S(2)}) collective-permute-start(f32[38,152]{1,0:T(8,128)S(1)} %get-tuple-element.14), channel_id=1, source_target_pairs={{0,127},{1,0},{2,1},{3,2},{4,3},{5,4},{6,5},{7,6},{8,7},{9,8},{10,... | collective-permute-start | bytes 69320 | tf_op jit(solution)/shard_map/ppermute | solution.py:233
  34.2 34.2 %copy-start.10 = (bf16[128,128]{1,0:T(8,128)(2,1)S(1)}, bf16[128,128]{1,0:T(8,128)(2,1)}, u32[]{:S(2)}) copy-start(bf16[128,128]{1,0:T(8,128)(2,1)} %constant.37.clone.fold_ref) | copy-start | bytes 98308
  36.7 21.6 %all-to-all-start.1 = ((bf16[128,24,128]{2,1,0:T(8,128)(2,1)}), bf16[128,24,128]{2,1,0:T(8,128)(2,1)S(1)}, u32[]{:S(2)}, u32[]{:S(2)}) async-start(bf16[128,24,128]{2,1,0:T(8,128)(2,1)} %bitcast.4), calls=%async_computation.1 | async-start | bytes 1572864 | tf_op jit(solution)/shard_map/all_to_all | solution.py:239
  41.9 42.3 %copy-start.6 = (f32[152,152]{1,0:T(8,128)S(1)}, f32[152,152]{1,0:T(8,128)}, u32[]{:S(2)}) copy-start(f32[152,152]{1,0:T(8,128)} %c2e_ref.1) | copy-start | bytes 277252
  41.9 42.3 %copy-start.11 = (bf16[64,152]{1,0:T(8,128)(2,1)S(1)}, bf16[64,152]{1,0:T(8,128)(2,1)}, u32[]{:S(2)}) copy-start(bf16[64,152]{1,0:T(8,128)(2,1)} %coarse_ref.1) | copy-start | bytes 58372
  58.3 25.9 %all-to-all-start = ((bf16[128,24,128]{2,1,0:T(8,128)(2,1)}), bf16[128,24,128]{2,1,0:T(8,128)(2,1)S(1)}, u32[]{:S(2)}, u32[]{:S(2)}) async-start(bf16[128,24,128]{2,1,0:T(8,128)(2,1)} %bitcast.2), calls=%async_computation | async-start | bytes 1572864 | tf_op jit(solution)/shard_map/all_to_all | solution.py:239
  86.1 8.6 %collective-permute-start.1 = (bf16[38,152]{1,0:T(8,128)(2,1)S(1)}, bf16[38,152]{1,0:T(8,128)(2,1)S(1)}, u32[]{:S(2)}, u32[]{:S(2)}) collective-permute-start(bf16[38,152]{1,0:T(8,128)(2,1)S(1)} %get-tuple-element.23), channel_id=1, source_target_pairs={{0,1},{1,2},{2,3},{3,4},{4,5},{5,6},{6,7},{7,8},{8,9},{9,10},{10,1... | collective-permute-start | bytes 34664 | tf_op jit(solution)/shard_map/ppermute | solution.py:233
